TPU v7x, 32 devices: a whole 2x2x4 slice. The times are simulated.
32 devices in a mesh: seq: 16 (over z, y, x), head: 2 (over core).
Axes of the slice: x: 2, y: 2, z: 4, core: 2. Of those that a mesh axis runs over, the one named last changes fastest.
Arguments:
- video_query: bfloat16 [8192, 3072], P('seq', 'head'), as said below
- video_value: bfloat16 [8192, 3072], P('seq', 'head'), may hold values from -12 to 12
- audio_key: bfloat16 [4096, 3072], P('seq', 'head'), as said below
- audio_value: bfloat16 [4096, 3072], P('seq', 'head'), may hold values from -12 to 12
- video_proj: bfloat16 [3072, 3072], P('head'), may hold values from -0.109375 to 0.109375
- audio_proj: bfloat16 [3072, 3072], P('head'), may hold values from -0.109375 to 0.109375
- pair_first: int32 [16], replicated, may hold values from 0 to 15, as said below
- pair_count: int32 [16], replicated, may hold values from 1 to 5, as said below
Outputs:
- video_out: bfloat16 [8192, 3072], P('seq', 'head')
- audio_out: bfloat16 [4096, 3072], P('seq', 'head')
Inputs may be any that keep to these rules, and one draw needn't show every extreme that they name: Video block b pairs with the audio blocks pair_first[b] to pair_first[b] + pair_count[b] - 1; these lie within b - 2 to b + 2, inside 0 to 15, and always include block b. `pair_count`: some video block pairs with 5 audio blocks in every draw. `video_query`: entries lie within -8 to 8. `audio_key`: entries lie within -8 to 8.
All inputs are finite; a program needn't handle non-finite values.
Results may differ from a plain program's by a relative error of at most 0.0052.
Values may be sent and summed in bfloat16 or wider, within the bound.
A program may use at most 192 MiB of HBM per device.

v0:
```python
import math

import jax
import jax.numpy as jnp
from jax import lax
from jax.sharding import PartitionSpec as P

HEAD_DIM = 128
HALF = 2


NEG = -1e30


def shifted(x, axis, by):
    size = lax.axis_size(axis)
    pairs = [(i, i + by) for i in range(size) if 0 <= i + by < size]
    return lax.ppermute(x, axis, pairs)


def tile_scores(query, keys):
    return jnp.einsum("vhe,ahe->hva", query, keys, preferred_element_type=jnp.float32) / math.sqrt(
        HEAD_DIM
    )


def row_piece(scores, values):
    top = jnp.max(scores, axis=2)
    expo = jnp.exp(scores - top[:, :, None])
    total = jnp.sum(expo, axis=2)
    out = jnp.einsum(
        "hva,ahe->vhe", expo.astype(jnp.bfloat16), values, preferred_element_type=jnp.float32
    )
    return (top, total, out)


def col_piece(scores, values):
    top = jnp.max(scores, axis=1)
    expo = jnp.exp(scores - top[:, None, :])
    total = jnp.sum(expo, axis=1)
    out = jnp.einsum(
        "hva,vhe->ahe", expo.astype(jnp.bfloat16), values, preferred_element_type=jnp.float32
    )
    return (top, total, out)


def combine(acc, part):
    top_a, total_a, out_a = acc
    top_b, total_b, out_b = part
    top = jnp.maximum(top_a, top_b)
    old = jnp.exp(top_a - top)
    new = jnp.exp(top_b - top)
    return (
        top,
        total_a * old + total_b * new,
        out_a * old.T[:, :, None] + out_b * new.T[:, :, None],
    )


def empty_acc(heads, rows):
    return (
        jnp.full((heads, rows), NEG, jnp.float32),
        jnp.zeros((heads, rows), jnp.float32),
        jnp.zeros((rows, heads, HEAD_DIM), jnp.float32),
    )


def finish(acc):
    top, total, out = acc
    result = (out / total.T[:, :, None]).astype(jnp.bfloat16)
    return result.reshape(result.shape[0], result.shape[1] * result.shape[2])


def shards(
    video_query, video_value, audio_key, audio_value, video_proj, audio_proj, pair_first, pair_count
):
    heads = video_query.shape[1] // HEAD_DIM
    vid = video_query.shape[0]
    aud = audio_key.shape[0]
    nblocks = lax.axis_size("seq")
    me = lax.axis_index("seq")
    first = pair_first[me]
    count = pair_count[me]
    query = video_query.reshape(vid, heads, HEAD_DIM)
    own_keys = audio_key.reshape(aud, heads, HEAD_DIM)
    audio_pair = jnp.stack([audio_key, audio_value])
    video_pair = jnp.stack([video_query, video_value])
    video_acc = empty_acc(heads, vid)
    audio_acc = empty_acc(heads, aud)
    for offset in range(-HALF, HALF + 1):
        if offset == 0:
            arrived = audio_pair
        else:
            arrived = shifted(audio_pair, "seq", -offset)
        keys = arrived[0].reshape(aud, heads, HEAD_DIM)
        aud_vals = arrived[1].reshape(aud, heads, HEAD_DIM)
        target = me + offset
        valid = (target >= first) & (target < first + count)
        source = me - offset
        clipped = jnp.clip(source, 0, nblocks - 1)
        from_source = (
            (source >= 0)
            & (source < nblocks)
            & (pair_first[clipped] <= me)
            & (me < pair_first[clipped] + pair_count[clipped])
        )

        def video_side(unused):
            return row_piece(tile_scores(query, keys), aud_vals)

        def no_video(unused):
            return empty_acc(heads, vid)

        video_acc = combine(video_acc, lax.cond(valid, video_side, no_video, 0))
        if offset == 0:
            visiting = video_pair
        else:
            visiting = shifted(video_pair, "seq", offset)

        def audio_side(unused):
            visit_query = visiting[0].reshape(vid, heads, HEAD_DIM)
            visit_vals = visiting[1].reshape(vid, heads, HEAD_DIM)
            return col_piece(tile_scores(visit_query, own_keys), visit_vals)

        def no_audio(unused):
            return empty_acc(heads, aud)

        audio_acc = combine(audio_acc, lax.cond(from_source, audio_side, no_audio, 0))
    video_attn = finish(video_acc)
    audio_attn = finish(audio_acc)
    video_term = jnp.dot(video_attn, video_proj, preferred_element_type=jnp.float32)
    audio_term = jnp.dot(audio_attn, audio_proj, preferred_element_type=jnp.float32)
    video_sum, audio_sum = (
        lax.psum_scatter(video_term, "head", scatter_dimension=1, tiled=True),
        lax.psum_scatter(audio_term, "head", scatter_dimension=1, tiled=True),
    )
    return (video_sum.astype(jnp.bfloat16), audio_sum.astype(jnp.bfloat16))


def solution(mesh):
    in_specs = (
        P("seq", "head"),
        P("seq", "head"),
        P("seq", "head"),
        P("seq", "head"),
        P("head", None),
        P("head", None),
        P(),
        P(),
    )
    out_specs = (P("seq", "head"), P("seq", "head"))
    return jax.shard_map(shards, mesh=mesh, in_specs=in_specs, out_specs=out_specs, check_vma=False)
```

profile of v0, /device:TPU:13, one launch (start us, length us, event | category | flops | bytes accessed | tf_op | source)
XLA Modules:
  0.0 459.7 jit_solution(3204376758789304763)
XLA Ops:
  10.6 3.4 pad_maximum_fusion
  14.1 3.1 collective-permute-start.7
  17.2 3.1 collective-permute-start.6
  20.3 3.1 collective-permute-start.5
  23.4 3.0 collective-permute-start.4
  36.9 19.2 %conditional.17 = (f32[12,256]{1,0:T(8,128)S(1)}, f32[12,256]{1,0:T(8,128)S(1)}, f32[256,12,128]{0,2,1:T(8,128)}) conditional(s32[]{:T(128)} %convert_element_type.81, () %tuple.102, (bf16[512,1536]{1,0:T(8,128)(2,1)}, bf16[256,12,128]{0,2,1:T(8,128)(2,1)S(1)}, bf16[512,1536]{1,0:T(8,128)(2,1)}) %tuple.222), branch_computations={%region_29.30_spmd, %region_30.33_spmd} | conditional | flops 817883136 | bytes 59129964 | solution.py:128
  36.9 2.6 copy.74
  39.5 2.4 multiply_reduce_fusion.7
  44.6 2.6 copy.76
  47.2 5.8 %fusion.76 = f32[256,12,128]{2,0,1:T(8,128)} fusion(bf16[512,12,128]{0,2,1:T(8,128)(2,1)} %bitcast.154, f32[12,512,256]{2,1,0:T(8,128)} %copy-done, f32[12,256]{1,0:T(8,128)S(1)} %get-tuple-element.304), kind=kOutput, calls=%fused_computation.70 | convolution fusion | flops 407371776 | bytes 9449472 | tf_op jit(solution)/shard_map/cond/branch_1_fun/hva,vhe->ahe/dot_general | solution.py:41
  53.0 3.1 copy.137
  56.1 164.0 %collective-permute-done.7 = bf16[2,512,1536]{1,2,0:T(8,128)(2,1)} collective-permute-done((bf16[2,512,1536]{1,2,0:T(8,128)(2,1)}, bf16[2,512,1536]{1,2,0:T(8,128)(2,1)}, u32[]{:S(2)}, u32[]{:S(2)}) %collective-permute-start.7) | collective-permute-done | bytes 3145760 | tf_op jit(solution)/shard_map/ppermute | solution.py:18
  220.1 9.9 %conditional.19 = (f32[12,256]{1,0:T(8,128)S(1)}, f32[12,256]{1,0:T(8,128)S(1)}, f32[256,12,128]{0,2,1:T(8,128)}) conditional(s32[]{:T(128)} %convert_element_type.83, () %tuple.106, (bf16[2,512,1536]{1,2,0:T(8,128)(2,1)}, bf16[256,12,128]{0,2,1:T(8,128)(2,1)S(1)}) %tuple.223), branch_computations={%region_37.38_spmd, %region_38.41_spmd} | conditional | flops 817883136 | bytes 33964112 | solution.py:128
  220.1 2.1 fusion.143
  224.3 2.6 fusion.96
  226.9 3.0 copy.141
  230.0 10.1 %conditional.18 = (f32[12,256]{1,0:T(8,128)S(1)}, f32[12,256]{1,0:T(8,128)S(1)}, f32[256,12,128]{0,2,1:T(8,128)}) conditional(s32[]{:T(128)} %convert_element_type.82, () %tuple.104, (bf16[2,512,1536]{1,2,0:T(8,128)(2,1)}, bf16[256,12,128]{0,2,1:T(8,128)(2,1)S(1)}) %tuple.224), branch_computations={%region_33.34_spmd, %region_34.37_spmd} | conditional | flops 817883136 | bytes 33964112 | solution.py:128
  230.1 2.1 fusion.142
  234.4 2.6 fusion.86
  237.0 3.0 copy.139
  241.4 10.3 %conditional.15 = (f32[12,256]{1,0:T(8,128)S(1)}, f32[12,256]{1,0:T(8,128)S(1)}, f32[256,12,128]{0,2,1:T(8,128)}) conditional(s32[]{:T(128)} %convert_element_type.79, () %tuple.98, (bf16[2,512,1536]{1,2,0:T(8,128)(2,1)}, bf16[256,12,128]{0,2,1:T(8,128)(2,1)S(1)}) %tuple.226), branch_computations={%region_21.22_spmd, %region_22.25_spmd} | conditional | flops 817883136 | bytes 33964112 | solution.py:128
  241.8 2.1 fusion.140
  246.0 2.6 fusion.56
  248.6 3.0 copy.133
  251.7 4.8 %divide_convert_fusion.1 = bf16[256,12,128]{0,2,1:T(8,128)(2,1)S(1)} fusion(f32[256,12,128]{0,2,1:T(8,128)} %get-tuple-element.180, f32[256,12,128]{0,2,1:T(8,128)} %get-tuple-element.179, f32[256,12,128]{0,2,1:T(8,128)} %get-tuple-element.178, f32[256,12,128]{0,2,1:T(8,128)} %get-tuple-element.177, f32[256,12,128]{0,2,1:T(8,128)} %get-tuple-element.176, ...), kind=kLoop, calls=%fused_computation.93 | loop fusion | flops 6291456 | bytes 8785920 | tf_op jit(solution)/shard_map/convert_element_type | solution.py:70
  256.5 8.0 %fusion.147 = f32[256,3072]{1,0:T(8,128)} fusion(bf16[256,1536]{0,1:T(8,128)(2,1)S(1)} %bitcast.161, bf16[1536,3072]{1,0:T(8,128)(2,1)} %param.33), kind=kOutput, calls=%fused_computation.163 | convolution fusion | flops 2415919104 | bytes 13369344 | tf_op jit(solution)/shard_map/dot_general | solution.py:132
  266.8 2.4 pad_maximum_fusion.1
  271.2 4.2 collective-permute-start.2
  275.3 9.5 %collective-permute-start.1 = (bf16[2,256,1536]{1,2,0:T(8,128)(2,1)}, bf16[2,256,1536]{1,2,0:T(8,128)(2,1)}, u32[]{:S(2)}, u32[]{:S(2)}) collective-permute-start(bf16[2,256,1536]{1,2,0:T(8,128)(2,1)} %pad_maximum_fusion.1), channel_id=1, source_target_pairs={{0,2},{2,4},{4,6},{6,8},{8,10},{10,12},{12,14},{14,16},{16,18},{18... | collective-permute-start | bytes 4718600 | tf_op jit(solution)/shard_map/ppermute | solution.py:18
  284.8 4.3 collective-permute-start
  293.4 13.6 %conditional.12 = (f32[12,512]{1,0:T(8,128)S(1)}, f32[12,512]{1,0:T(8,128)S(1)}, f32[512,12,128]{0,2,1:T(8,128)}) conditional(s32[]{:T(128)} %convert_element_type.74, () %tuple.92, (bf16[512,12,128]{0,2,1:T(8,128)(2,1)S(1)}, bf16[256,12,128]{0,2,1:T(8,128)(2,1)S(1)}, bf16[256,1536]{1,0:T(8,128)(2,1)S(1)}) %tuple.228), branch_computations={%region_8.9_spmd, %region_9.12_spmd} | conditional | flops 817876992 | bytes 58490988 | solution.py:114
  297.6 5.9 %fusion.26 = f32[512,12,128]{2,0,1:T(8,128)} fusion(bf16[256,12,128]{0,2,1:T(8,128)(2,1)S(1)} %bitcast.162, f32[12,512,256]{1,2,0:T(8,128)} %copy-done.1, f32[12,512]{1,0:T(8,128)S(1)} %get-tuple-element.274), kind=kOutput, calls=%fused_computation.25 | convolution fusion | flops 407371776 | bytes 10248192 | tf_op jit(solution)/shard_map/cond/branch_1_fun/hva,ahe->vhe/dot_general | solution.py:31
  303.4 3.5 copy.127
  307.0 64.3 %collective-permute-done.3 = bf16[2,256,1536]{1,2,0:T(8,128)(2,1)} collective-permute-done((bf16[2,256,1536]{1,2,0:T(8,128)(2,1)}, bf16[2,256,1536]{1,2,0:T(8,128)(2,1)}, u32[]{:S(2)}, u32[]{:S(2)}) %collective-permute-start.3) | collective-permute-done | bytes 1572896 | tf_op jit(solution)/shard_map/ppermute | solution.py:18
  371.3 2.1 conditional.14
  371.3 2.1 broadcast.156.clone
  373.3 10.5 %conditional.13 = (f32[12,512]{1,0:T(8,128)S(1)}, f32[12,512]{1,0:T(8,128)S(1)}, f32[512,12,128]{0,2,1:T(8,128)}) conditional(s32[]{:T(128)} %convert_element_type.75, () %tuple.94, (bf16[2,256,1536]{1,2,0:T(8,128)(2,1)}, bf16[512,12,128]{0,2,1:T(8,128)(2,1)S(1)}) %tuple.219), branch_computations={%region_12.13_spmd, %region_13.16_spmd} | conditional | flops 817876992 | bytes 34898000 | solution.py:114
  377.2 3.1 fusion.36
  380.3 3.5 copy.129
  383.8 10.3 %conditional.11 = (f32[12,512]{1,0:T(8,128)S(1)}, f32[12,512]{1,0:T(8,128)S(1)}, f32[512,12,128]{0,2,1:T(8,128)}) conditional(s32[]{:T(128)} %convert_element_type.73, () %tuple.90, (bf16[2,256,1536]{1,2,0:T(8,128)(2,1)}, bf16[512,12,128]{0,2,1:T(8,128)(2,1)S(1)}) %tuple.220), branch_computations={%region_4.5_spmd, %region_5.8_spmd} | conditional | flops 817876992 | bytes 34898000 | solution.py:114
  387.5 3.1 fusion.16
  390.6 3.6 copy.125
  394.2 2.3 conditional.10
  396.6 7.0 %divide_convert_fusion = bf16[512,12,128]{0,2,1:T(8,128)(2,1)S(1)} fusion(f32[512,12,128]{0,2,1:T(8,128)} %get-tuple-element.175, f32[512,12,128]{0,2,1:T(8,128)} %get-tuple-element.174, f32[512,12,128]{0,2,1:T(8,128)} %get-tuple-element.173, f32[512,12,128]{0,2,1:T(8,128)} %get-tuple-element.172, f32[512,12,128]{0,2,1:T(8,128)} %get-tuple-element.171, ...), kind=kLoop, calls=%fused_computation.91 | loop fusion | flops 12582912 | bytes 17571840 | tf_op jit(solution)/shard_map/convert_element_type | solution.py:70
  403.7 10.7 %fusion.146 = f32[512,3072]{1,0:T(8,128)} fusion(bf16[512,1536]{0,1:T(8,128)(2,1)S(1)} %bitcast.172, bf16[1536,3072]{1,0:T(8,128)(2,1)} %param.32), kind=kOutput, calls=%fused_computation.162 | convolution fusion | flops 4831838208 | bytes 17301504 | tf_op jit(solution)/shard_map/dot_general | solution.py:131
  414.4 2.4 convert_element_type.85
  416.8 32.4 %reduce-scatter.3.cloned.1.call-done = f32[512,1536]{1,0:T(8,128)} async-done(((f32[512,3072]{1,0:T(8,128)}), f32[512,1536]{1,0:T(8,128)}) %reduce-scatter.3.cloned.1.call-update) | async-done | bytes 3145744 | tf_op jit(solution)/shard_map/reduce_scatter | solution.py:134
  449.2 3.2 convert_element_type.78
  (88 shorter events, 33.7 us)
Async XLA Ops:
  7.2 1.9 copy-start.2
  7.2 407.3 %reduce-scatter.5.cloned.1.call-start = ((), (), s32[]{:S(2)}) async-start(), calls=%async_computation.3 | async-start | bytes 4718592 | tf_op jit(solution)/shard_map/reduce_scatter | solution.py:135
  10.6 15.8 %copy-start.10 = (bf16[256,1536]{1,0:T(8,128)(2,1)S(1)}, bf16[256,1536]{1,0:T(8,128)(2,1)}, u32[]{:S(2)}) copy-start(bf16[256,1536]{1,0:T(8,128)(2,1)} %param.30) | copy-start | bytes 2359300
  10.6 16.1 %copy-start.25 = (s32[16]{0:T(128)S(1)}, s32[16]{0:T(128)}, u32[]{:S(2)}) copy-start(s32[16]{0:T(128)} %param.35) | copy-start | bytes 196
  10.6 16.1 %copy-start.26 = (s32[16]{0:T(128)S(1)}, s32[16]{0:T(128)}, u32[]{:S(2)}) copy-start(s32[16]{0:T(128)} %param.34) | copy-start | bytes 196
  14.1 206.0 %collective-permute-start.7 = (bf16[2,512,1536]{1,2,0:T(8,128)(2,1)}, bf16[2,512,1536]{1,2,0:T(8,128)(2,1)}, u32[]{:S(2)}, u32[]{:S(2)}) collective-permute-start(bf16[2,512,1536]{1,2,0:T(8,128)(2,1)} %pad_maximum_fusion), channel_id=1, source_target_pairs={{0,4},{2,6},{4,8},{6,10},{8,12},{10,14},{12,16},{14,18},{16,20},{1... | collective-permute-start | bytes 9437192 | tf_op jit(solution)/shard_map/ppermute | solution.py:18
  17.2 212.7 %collective-permute-start.6 = (bf16[2,512,1536]{1,2,0:T(8,128)(2,1)}, bf16[2,512,1536]{1,2,0:T(8,128)(2,1)}, u32[]{:S(2)}, u32[]{:S(2)}) collective-permute-start(bf16[2,512,1536]{1,2,0:T(8,128)(2,1)} %pad_maximum_fusion), channel_id=1, source_target_pairs={{0,2},{2,4},{4,6},{6,8},{8,10},{10,12},{12,14},{14,16},{16,18},{18... | collective-permute-start | bytes 9437192 | tf_op jit(solution)/shard_map/ppermute | solution.py:18
  20.3 219.7 %collective-permute-start.5 = (bf16[2,512,1536]{1,2,0:T(8,128)(2,1)}, bf16[2,512,1536]{1,2,0:T(8,128)(2,1)}, u32[]{:S(2)}, u32[]{:S(2)}) collective-permute-start(bf16[2,512,1536]{1,2,0:T(8,128)(2,1)} %pad_maximum_fusion), channel_id=1, source_target_pairs={{2,0},{4,2},{6,4},{8,6},{10,8},{12,10},{14,12},{16,14},{18,16},{20... | collective-permute-start | bytes 9437192 | tf_op jit(solution)/shard_map/ppermute | solution.py:18
  23.4 218.0 %collective-permute-start.4 = (bf16[2,512,1536]{1,2,0:T(8,128)(2,1)}, bf16[2,512,1536]{1,2,0:T(8,128)(2,1)}, u32[]{:S(2)}, u32[]{:S(2)}) collective-permute-start(bf16[2,512,1536]{1,2,0:T(8,128)(2,1)} %pad_maximum_fusion), channel_id=1, source_target_pairs={{4,0},{6,2},{8,4},{10,6},{12,8},{14,10},{16,12},{18,14},{20,16},{2... | collective-permute-start | bytes 9437192 | tf_op jit(solution)/shard_map/ppermute | solution.py:18
  41.9 2.7 copy-start
  41.9 5.2 %copy-start.15 = (f32[12,256]{1,0:T(8,128)}, f32[12,256]{1,0:T(8,128)S(1)}, u32[]{:S(2)}) copy-start(f32[12,256]{1,0:T(8,128)S(1)} %get-tuple-element.304) | copy-start | bytes 36868 | tf_op jit(solution)/shard_map/cond
  53.0 3.1 copy-start.16
  223.2 1.1 copy-start.21
  226.9 3.0 copy-start.22
  233.3 1.1 copy-start.23
  237.0 3.1 copy-start.24
  244.9 1.1 copy-start.19
  248.6 3.0 copy-start.20
  264.5 1.1 copy-start.3
  264.6 184.7 %reduce-scatter.3.cloned.1.call-start = ((), (), s32[]{:S(2)}) async-start(), calls=%async_computation.2 | async-start | bytes 9437184 | tf_op jit(solution)/shard_map/reduce_scatter | solution.py:134
  269.2 102.0 %collective-permute-start.3 = (bf16[2,256,1536]{1,2,0:T(8,128)(2,1)}, bf16[2,256,1536]{1,2,0:T(8,128)(2,1)}, u32[]{:S(2)}, u32[]{:S(2)}) collective-permute-start(bf16[2,256,1536]{1,2,0:T(8,128)(2,1)} %pad_maximum_fusion.1), channel_id=1, source_target_pairs={{4,0},{6,2},{8,4},{10,6},{12,8},{14,10},{16,12},{18,14},{20,16},{2... | collective-permute-start | bytes 4718600 | tf_op jit(solution)/shard_map/ppermute | solution.py:18
  271.2 102.2 %collective-permute-start.2 = (bf16[2,256,1536]{1,2,0:T(8,128)(2,1)}, bf16[2,256,1536]{1,2,0:T(8,128)(2,1)}, u32[]{:S(2)}, u32[]{:S(2)}) collective-permute-start(bf16[2,256,1536]{1,2,0:T(8,128)(2,1)} %pad_maximum_fusion.1), channel_id=1, source_target_pairs={{2,0},{4,2},{6,4},{8,6},{10,8},{12,10},{14,12},{16,14},{18,16},{20... | collective-permute-start | bytes 4718600 | tf_op jit(solution)/shard_map/ppermute | solution.py:18
  275.3 108.5 %collective-permute-start.1 = (bf16[2,256,1536]{1,2,0:T(8,128)(2,1)}, bf16[2,256,1536]{1,2,0:T(8,128)(2,1)}, u32[]{:S(2)}, u32[]{:S(2)}) collective-permute-start(bf16[2,256,1536]{1,2,0:T(8,128)(2,1)} %pad_maximum_fusion.1), channel_id=1, source_target_pairs={{0,2},{2,4},{4,6},{6,8},{8,10},{10,12},{12,14},{14,16},{16,18},{18... | collective-permute-start | bytes 4718600 | tf_op jit(solution)/shard_map/ppermute | solution.py:18
  284.8 109.4 %collective-permute-start = (bf16[2,256,1536]{1,2,0:T(8,128)(2,1)}, bf16[2,256,1536]{1,2,0:T(8,128)(2,1)}, u32[]{:S(2)}, u32[]{:S(2)}) collective-permute-start(bf16[2,256,1536]{1,2,0:T(8,128)(2,1)} %pad_maximum_fusion.1), channel_id=1, source_target_pairs={{0,4},{2,6},{4,8},{6,10},{8,12},{10,14},{12,16},{14,18},{16,20},{1... | collective-permute-start | bytes 4718600 | tf_op jit(solution)/shard_map/ppermute | solution.py:18
  294.6 2.7 copy-start.1
  294.6 2.9 copy-start.4
  303.4 3.5 copy-start.5
  376.1 1.1 copy-start.13
  380.3 3.5 copy-start.14
  386.4 1.1 copy-start.6
  390.6 3.6 copy-start.7
Sparse Core Ops, SparseCore 0:
  264.7 20.1 reduce-scatter.4
  414.5 34.6 reduce-scatter.2
where the time goes:
time: 463 us; the launch traced here: 460 us
  waiting for transfers between devices  261 us (56%)
  matrix products  53.2 us (11%)
  local copies, waits for them, and re-layouts  52.8 us (11%)
  starting transfers between devices  32.2 us (7%)
  other arithmetic  30.8 us (7%)
  between operations  28.4 us (6%)
    ppermute x8, waiting for transfers between devices, shifted(): return lax.ppermute(x, axis, pairs)  228 us
    reduce_scatter x1, waiting for transfers between devices, shards(): lax.psum_scatter(video_term, 'head', scatter_dimension=1, tiled=True)  32.4 us
    ppermute x8, starting transfers between devices, shifted(): return lax.ppermute(x, axis, pairs)  32.1 us
    dot_general x4, matrix products, col_piece(): jnp.einsum('hva,vhe->ahe', expo.astype(jnp.bfloat16), values, preferred_e...  13.7 us
    cond x4, local copies, waits for them, and re-layouts, shards(): lax.cond(from_source, audio_side, no_audio, 0)  12.2 us
    dot_general x3, matrix products, row_piece(): jnp.einsum('hva,ahe->vhe', expo.astype(jnp.bfloat16), values, preferred_e...  12.1 us
    convert_element_type x2, other arithmetic, finish(): result = (out / total.T[:, :, None]).astype(jnp.bfloat16)  11.8 us
    another operation x12, local copies, waits for them, and re-layouts  10.9 us
  transfers between devices with their start and end apart: 10, of which 3 were waited for; matrix products, arithmetic and copies ran while one was open for 22% of the time, Pallas kernels for 0%

commit v1 on v0

--- a/solution.py
+++ b/solution.py
@@ -3,6 +3,8 @@
 import jax
 import jax.numpy as jnp
 from jax import lax
+from jax.experimental import pallas as pl
+from jax.experimental.pallas import tpu as pltpu
 from jax.sharding import PartitionSpec as P
 
 HEAD_DIM = 128
@@ -71,7 +73,7 @@
     return result.reshape(result.shape[0], result.shape[1] * result.shape[2])
 
 
-def shards(
+def safe_shards(
     video_query, video_value, audio_key, audio_value, video_proj, audio_proj, pair_first, pair_count
 ):
     heads = video_query.shape[1] // HEAD_DIM
@@ -137,6 +139,185 @@
     return (video_sum.astype(jnp.bfloat16), audio_sum.astype(jnp.bfloat16))
 
 
+GROUP = 4
+SCALE = 1.4426950408889634 / math.sqrt(HEAD_DIM)
+LOW, HIGH = 1e-25, 1e25
+
+
+def pair_kernel(valid, x0, x1, x2, x3, prev, after, o_ref, u_ref, halo_ref, bad_ref, q, k, av, vv, o_acc, u_acc):
+    vid = q.shape[1]
+    aud = k.shape[1]
+    av[:, :, HEAD_DIM:] = jnp.ones((2 * GROUP, aud, HEAD_DIM), jnp.bfloat16)
+    vv[:, :, HEAD_DIM:] = jnp.ones((GROUP, vid, HEAD_DIM), jnp.bfloat16)
+    for slot, x in enumerate((x0, x1, x2, x3)):
+        q[slot] = x[:vid]
+        vv[slot, :, :HEAD_DIM] = x[vid : 2 * vid]
+        k[slot] = x[2 * vid : 2 * vid + aud]
+        av[slot, :, :HEAD_DIM] = x[2 * vid + aud :]
+    for slot, (x, at) in enumerate(((prev, 0), (prev, 1), (after, 0), (after, 1))):
+        k[GROUP + slot] = x[at, :aud]
+        av[GROUP + slot, :, :HEAD_DIM] = x[at, aud:]
+    o_acc[...] = jnp.zeros_like(o_acc)
+    u_acc[...] = jnp.zeros_like(u_acc)
+
+    def step(pair, carry):
+        row = pair // (2 * GROUP)
+        col = pair % (2 * GROUP)
+
+        @pl.when(valid[pair] != 0)
+        def _():
+            scores = lax.dot_general(
+                q[row], k[col], (((1,), (1,)), ((), ())), preferred_element_type=jnp.float32
+            )
+            weights = jnp.exp2(scores * SCALE).astype(jnp.bfloat16)
+            o_acc[row] += jnp.dot(weights, av[col], preferred_element_type=jnp.float32)
+            u_acc[col] += lax.dot_general(
+                weights, vv[row], (((0,), (0,)), ((), ())), preferred_element_type=jnp.float32
+            )
+
+        return carry
+
+    lax.fori_loop(0, 2 * GROUP * GROUP, step, 0)
+    bad = jnp.zeros((8, HEAD_DIM), jnp.float32)
+    for slot in range(GROUP):
+        total = o_acc[slot, :, HEAD_DIM:]
+        o_ref[slot] = (o_acc[slot, :, :HEAD_DIM] / total).astype(jnp.bfloat16)
+        wrong = jnp.where((total >= LOW) & (total <= HIGH), 0.0, 1.0)
+        bad = jnp.maximum(bad, jnp.max(wrong.reshape(vid // 8, 8, HEAD_DIM), axis=0))
+        u_ref[slot] = u_acc[slot]
+        halo_ref[slot] = u_acc[GROUP + slot].astype(jnp.bfloat16)
+    bad_ref[...] = bad
+
+
+def pair_call(valid, parts, prev, after, vid, aud):
+    vmem = pl.BlockSpec(memory_space=pltpu.VMEM)
+    wide = 2 * HEAD_DIM
+    tiles = 4 * GROUP
+    return pl.pallas_call(
+        pair_kernel,
+        in_specs=[pl.BlockSpec(memory_space=pltpu.SMEM)] + [vmem] * 6,
+        out_specs=[vmem] * 4,
+        out_shape=[
+            jax.ShapeDtypeStruct((GROUP, vid, HEAD_DIM), jnp.bfloat16),
+            jax.ShapeDtypeStruct((GROUP, aud, wide), jnp.float32),
+            jax.ShapeDtypeStruct((GROUP, aud, wide), jnp.bfloat16),
+            jax.ShapeDtypeStruct((8, HEAD_DIM), jnp.float32),
+        ],
+        scratch_shapes=[
+            pltpu.VMEM((GROUP, vid, HEAD_DIM), jnp.bfloat16),
+            pltpu.VMEM((2 * GROUP, aud, HEAD_DIM), jnp.bfloat16),
+            pltpu.VMEM((2 * GROUP, aud, wide), jnp.bfloat16),
+            pltpu.VMEM((GROUP, vid, wide), jnp.bfloat16),
+            pltpu.VMEM((GROUP, vid, wide), jnp.float32),
+            pltpu.VMEM((2 * GROUP, aud, wide), jnp.float32),
+        ],
+        compiler_params=pltpu.CompilerParams(vmem_limit_bytes=48 * 1024 * 1024),
+        cost_estimate=pl.CostEstimate(
+            flops=tiles * 12 * vid * aud * HEAD_DIM,
+            bytes_accessed=8 * 1024 * 1024,
+            transcendentals=tiles * vid * aud,
+        ),
+    )(valid, *parts, prev, after)
+
+
+def swap(x, distance):
+    size = lax.axis_size("seq")
+    return lax.ppermute(x, "seq", [(i, i ^ distance) for i in range(size)])
+
+
+def pick(x, index):
+    return lax.dynamic_index_in_dim(x, index, 0, keepdims=False)
+
+
+def in_order(parts, place):
+    odd = (place & 1) == 1
+    parts = [jnp.where(odd, parts[d ^ 1], parts[d]) for d in range(GROUP)]
+    high = (place & 2) == 2
+    return [jnp.where(high, parts[d ^ 2], parts[d]) for d in range(GROUP)]
+
+
+def fast_attention(video_query, video_value, audio_key, audio_value, pair_first, pair_count):
+    vid, width = video_query.shape
+    aud = audio_key.shape[0]
+    heads = width // HEAD_DIM
+    each = heads // GROUP
+    me = lax.axis_index("seq")
+    place = me % GROUP
+    base = me - place
+    slots = [place ^ d for d in range(GROUP)]
+    video_blocks = jnp.stack([base + s for s in slots])
+    audio_blocks = jnp.stack([base + s for s in slots] + [base - 2, base - 1, base + GROUP, base + GROUP + 1])
+    first = pair_first[video_blocks][:, None]
+    count = pair_count[video_blocks][:, None]
+    valid = (audio_blocks[None, :] >= first) & (audio_blocks[None, :] < first + count)
+    valid = valid.astype(jnp.int32).reshape(-1)
+
+    video_pieces = [[] for _ in range(GROUP)]
+    audio_pieces = [[] for _ in range(GROUP)]
+    bads = []
+    for t in range(each):
+        parts = []
+        for d in range(GROUP):
+            column = (slots[d] * each + t) * HEAD_DIM
+            piece = jnp.concatenate(
+                [
+                    lax.dynamic_slice_in_dim(x, column, HEAD_DIM, 1)
+                    for x in (video_query, video_value, audio_key, audio_value)
+                ]
+            )
+            parts.append(piece if d == 0 else swap(piece, d))
+        keyed = in_order([x[2 * vid :] for x in parts], place)
+        prev = shifted(jnp.stack(keyed[2:]), "seq", GROUP)
+        after = shifted(jnp.stack(keyed[:2]), "seq", -GROUP)
+        out, own, halo, bad = pair_call(valid, parts, prev, after, vid, aud)
+        bads.append(jnp.max(bad))
+        for d in range(GROUP):
+            video_pieces[d].append(out[d] if d == 0 else swap(out[d], d))
+        from_after = shifted(halo[:2], "seq", -GROUP)
+        from_prev = shifted(halo[2:], "seq", GROUP)
+        extra = jnp.concatenate([from_prev, from_after])
+        for d in range(GROUP):
+            both = own[d] + pick(extra, slots[d]).astype(jnp.float32)
+            total = both[:, HEAD_DIM:]
+            bads.append(jnp.max(jnp.where((total >= LOW) & (total <= HIGH), 0.0, 1.0)))
+            piece = (both[:, :HEAD_DIM] / total).astype(jnp.bfloat16)
+            audio_pieces[d].append(piece if d == 0 else swap(piece, d))
+    video_attn = jnp.concatenate(
+        in_order([jnp.concatenate(p, axis=1) for p in video_pieces], place), axis=1
+    )
+    audio_attn = jnp.concatenate(
+        in_order([jnp.concatenate(p, axis=1) for p in audio_pieces], place), axis=1
+    )
+    return video_attn, audio_attn, jnp.max(jnp.stack(bads))
+
+
+def shards(
+    video_query, video_value, audio_key, audio_value, video_proj, audio_proj, pair_first, pair_count
+):
+    video_attn, audio_attn, bad = fast_attention(
+        video_query, video_value, audio_key, audio_value, pair_first, pair_count
+    )
+    bad = lax.pmax(bad, ("seq", "head"))
+    half = video_proj.shape[1] // 2
+    core = lax.axis_index("head")
+
+    def project(attn, proj):
+        theirs = lax.dynamic_slice_in_dim(proj, (1 - core) * half, half, 1)
+        mine = lax.dynamic_slice_in_dim(proj, core * half, half, 1)
+        away = jnp.dot(attn, theirs, preferred_element_type=jnp.float32)
+        arrived = lax.ppermute(away, "head", [(0, 1), (1, 0)])
+        return (jnp.dot(attn, mine, preferred_element_type=jnp.float32) + arrived).astype(jnp.bfloat16)
+
+    video_out = project(video_attn, video_proj)
+    audio_out = project(audio_attn, audio_proj)
+    return lax.cond(
+        bad > 0,
+        lambda args: safe_shards(*args),
+        lambda args: (video_out, audio_out),
+        (video_query, video_value, audio_key, audio_value, video_proj, audio_proj, pair_first, pair_count),
+    )
+
+
 def solution(mesh):
     in_specs = (
         P("seq", "head"),

time: 463 us -> 701 us (1.51); the launches traced: 460 us -> 688 us
  waiting for transfers between devices: 261 us -> 343 us
  starting transfers between devices: 32.2 us -> 97.5 us
  blocking collectives: 0 us -> 37.8 us
  Pallas kernels: 0 us -> 20.2 us
  loops' own time: 1.52 us -> 18.5 us
  other arithmetic: 30.8 us -> 47.6 us
  local copies, waits for them, and re-layouts: 52.8 us -> 41.5 us
    ppermute x0 -> x29, waiting for transfers between devices: none -> 53.7 us  [the longest x27 53.7 us: swap(): return lax.ppermute(x, 'seq', [(i, i ^ distance) for i in range(size)])]
    pmax x0 -> x1, blocking collectives: none -> 37.8 us  [shards(): bad = lax.pmax(bad, ('seq', 'head'))]
    ppermute x8 -> x20, starting transfers between devices: 32.1 us -> 67.6 us  [shifted(): return lax.ppermute(x, axis, pairs)]
    ppermute x0 -> x29, starting transfers between devices: none -> 29.8 us  [the longest x27 19.8 us: swap(): return lax.ppermute(x, 'seq', [(i, i ^ distance) for i in range(size)])]
    dot_general x2 -> x6, matrix products: 18.8 us -> 40.6 us  [the longest x2 12 us: project(): jnp.dot(attn, mine, preferred_element_type=jnp.float32) + arrived]
    pallas_call x0 -> x3, Pallas kernels: none -> 20.2 us  [pair_call(): pl.pallas_call(pair_kernel, in_specs=[pl.BlockSpec(memory_space=pltpu.SME...]
    reduce_scatter x2, waiting for transfers between devices: 32.4 us -> 50.4 us  [the longest x1 50.3 us: safe_shards(): lax.psum_scatter(video_term, 'head', scatter_dimension=1, tiled=True)]
    another operation x10 -> x11, loops' own time: 1.52 us -> 18.5 us  [the longest x1 14.8 us: shards(): lax.cond(bad > 0, lambda args: safe_shards(*args), lambda args: (video_ou...]
  transfers between devices with their start and end apart: 10 -> 51, of which waited for: 3 -> 20; matrix products, arithmetic and copies ran while one was open for 22% -> 15% of each run, Pallas kernels for 0% -> 3%
where the time goes in v1:
time: 701 us; the launch traced here: 688 us
  waiting for transfers between devices  343 us (49%)
  starting transfers between devices  97.5 us (14%)
  matrix products  55.6 us (8%)
  other arithmetic  47.6 us (7%)
  local copies, waits for them, and re-layouts  41.5 us (6%)
  blocking collectives  37.8 us (5%)
  between operations  26.1 us (4%)
  Pallas kernels  20.2 us (3%)
  loops' own time  18.5 us (3%)
    ppermute x20, waiting for transfers between devices, shifted(): return lax.ppermute(x, axis, pairs)  239 us
    ppermute x20, starting transfers between devices, shifted(): return lax.ppermute(x, axis, pairs)  67.6 us
    ppermute x27, waiting for transfers between devices, swap(): return lax.ppermute(x, 'seq', [(i, i ^ distance) for i in range(size)])  53.7 us
    reduce_scatter x1, waiting for transfers between devices, safe_shards(): lax.psum_scatter(video_term, 'head', scatter_dimension=1, tiled=True)  50.3 us
    pmax x1, blocking collectives, shards(): bad = lax.pmax(bad, ('seq', 'head'))  37.8 us
    pallas_call x3, Pallas kernels, pair_call(): pl.pallas_call(pair_kernel, in_specs=[pl.BlockSpec(memory_space=pltpu.SME...  20.2 us
    ppermute x27, starting transfers between devices, swap(): return lax.ppermute(x, 'seq', [(i, i ^ distance) for i in range(size)])  19.8 us
    another operation x22, local copies, waits for them, and re-layouts  16 us
  transfers between devices with their start and end apart: 51, of which 20 were waited for; matrix products, arithmetic and copies ran while one was open for 15% of the time, Pallas kernels for 3%

profile of v1, /device:TPU:13, one launch (start us, length us, event | category | flops | bytes accessed | tf_op | source)
XLA Modules:
  0.0 687.8 jit_solution(557766271889167573)
XLA Ops:
  7.3 2.7 constant_dynamic-slice_fusion
  32.6 7.0 %collective-permute-done.15.x1 = bf16[1536,128]{1,0:T(8,128)(2,1)S(1)} collective-permute-done((bf16[1536,128]{1,0:T(8,128)(2,1)}, bf16[1536,128]{1,0:T(8,128)(2,1)S(1)}, u32[]{:S(2)}, u32[]{:S(2)}) %collective-permute-start.15) | collective-permute-done | bytes 393248 | tf_op jit(solution)/shard_map/ppermute | solution.py:225
  40.7 8.2 %collective-permute-done.16.x2 = bf16[1536,128]{1,0:T(8,128)(2,1)S(1)} collective-permute-done((bf16[1536,128]{1,0:T(8,128)(2,1)}, bf16[1536,128]{1,0:T(8,128)(2,1)S(1)}, u32[]{:S(2)}, u32[]{:S(2)}) %collective-permute-start.16) | collective-permute-done | bytes 393248 | tf_op jit(solution)/shard_map/ppermute | solution.py:225
  48.9 3.2 collective-permute-start.11
  56.4 3.2 collective-permute-start.18
  59.6 6.8 collective-permute-done.23.x2
  68.7 3.2 collective-permute-start.25
  74.1 6.7 shard_map.99
  80.9 5.3 collective-permute-start.13
  88.2 6.7 shard_map.100
  95.0 5.5 collective-permute-start.20
  100.4 6.7 shard_map.101
  107.5 4.6 collective-permute-done.29
  113.7 3.1 collective-permute-done.35
  119.1 4.1 collective-permute-done.31
  123.4 5.8 collective-permute-done.34
  136.0 7.2 %fusion.138 = f32[512,1536]{1,0:T(8,128)} fusion(bf16[1536,3072]{1,0:T(8,128)(2,1)} %param.34, s32[]{:T(128)S(6)} %select_n.420, bf16[512,384]{1,0:T(8,128)(2,1)S(1)} %get-tuple-element.296, bf16[512,384]{1,0:T(8,128)(2,1)S(1)} %get-tuple-element.295, bf16[512,384]{1,0:T(8,128)(2,1)S(1)} %get-tuple-element.294, bf16[512,384]{1,0:T(8,128)(2,1)S(1)} %get-tuple-element.293), kind=kOutput, calls=%fused_computation.158 | convolution fusion | flops 2422210560 | bytes 9437188 | tf_op jit(solution)/shard_map/dot_general | solution.py:307
  143.2 3.4 collective-permute-start.28
  146.6 6.8 collective-permute-start.38
  167.1 2.8 collective-permute-done.42
  182.3 3.2 collective-permute-start.48
  197.1 37.8 %pmax.7 = f32[]{:T(128)} all-reduce(f32[]{:T(128)S(6)} %reduce_max.299), channel_id=1, replica_groups=mesh['seq'=16,'head'=2] {'seq','head'}, use_global_device_ids=true, to_apply=%region_15.16 | all-reduce | flops 1 | bytes 8 | tf_op jit(solution)/shard_map/pmax | solution.py:300
  235.6 5.5 fusion.151
  241.1 6.5 fusion.145
  247.7 432.8 %conditional.11 = ((bf16[512,1536]{1,0:T(8,128)(2,1)}, bf16[256,1536]{1,0:T(8,128)(2,1)})) conditional(s32[]{:T(128)} %convert_element_type.186, (bf16[512,1536]{1,0:T(8,128)(2,1)}, bf16[256,1536]{1,0:T(8,128)(2,1)}) %tuple.94, (s32[16]{0:T(128)S(1)}, s32[16]{0:T(128)S(1)}, bf16[512,1536]{1,0:T(8,128)(2,1)S(1)}, bf16[256,1536]{1,0:T(8,128)(2,1)}, ...), branch_computations={%region_16.17_spmd, %region_17.60_spmd} | conditional | flops 15449275392 | bytes 549361472 | solution.py:313
  252.2 2.7 collective-permute-start.7
  255.0 3.3 collective-permute-start.6
  258.3 2.9 collective-permute-start.5
  261.2 3.4 collective-permute-start.4
  276.3 8.3 %conditional.7 = (f32[12,256]{1,0:T(8,128)S(1)}, f32[12,256]{1,0:T(8,128)S(1)}, f32[256,12,128]{0,2,1:T(8,128)}) conditional(s32[]{:T(128)} %convert_element_type.138, () %tuple.84, (bf16[512,1536]{0,1:T(8,128)(2,1)S(1)}, bf16[256,12,128]{0,2,1:T(8,128)(2,1)S(1)}, bf16[512,1536]{0,1:T(8,128)(2,1)}) %tuple.339), branch_computations={%region_47.47_spmd, %region_48.50_spmd} | conditional | flops 817883136 | bytes 33964140 | solution.py:130
  281.6 3.0 copy.136
  284.6 171.9 %collective-permute-done.7 = bf16[2,512,1536]{1,2,0:T(8,128)(2,1)} collective-permute-done((bf16[2,512,1536]{1,2,0:T(8,128)(2,1)}, bf16[2,512,1536]{1,2,0:T(8,128)(2,1)}, u32[]{:S(2)}, u32[]{:S(2)}) %collective-permute-start.7) | collective-permute-done | bytes 3145760 | tf_op jit(solution)/shard_map/cond/branch_1_fun/ppermute | solution.py:20
  459.5 10.0 %conditional.6 = (f32[12,256]{1,0:T(8,128)S(1)}, f32[12,256]{1,0:T(8,128)S(1)}, f32[256,12,128]{0,2,1:T(8,128)}) conditional(s32[]{:T(128)} %convert_element_type.137, () %tuple.82, (bf16[2,512,1536]{1,2,0:T(8,128)(2,1)}, bf16[256,12,128]{0,2,1:T(8,128)(2,1)S(1)}) %tuple.336), branch_computations={%region_43.43_spmd, %region_44.46_spmd} | conditional | flops 817883136 | bytes 33964112 | solution.py:130
  466.3 3.1 copy.134
  469.5 10.1 %conditional.5 = (f32[12,256]{1,0:T(8,128)S(1)}, f32[12,256]{1,0:T(8,128)S(1)}, f32[256,12,128]{0,2,1:T(8,128)}) conditional(s32[]{:T(128)} %convert_element_type.136, () %tuple.80, (bf16[2,512,1536]{1,2,0:T(8,128)(2,1)}, bf16[256,12,128]{0,2,1:T(8,128)(2,1)S(1)}) %tuple.337), branch_computations={%region_39.39_spmd, %region_40.42_spmd} | conditional | flops 817883136 | bytes 33964112 | solution.py:130
  476.5 3.1 copy.132
  479.6 4.8 divide_convert_fusion.1
  484.4 8.1 %fusion.191 = f32[256,3072]{1,0:T(8,128)} fusion(bf16[256,1536]{0,1:T(8,128)(2,1)S(1)} %bitcast.251, bf16[1536,3072]{1,0:T(8,128)(2,1)} %get-tuple-element.144), kind=kOutput, calls=%fused_computation.389 | convolution fusion | flops 2415919104 | bytes 13369344 | tf_op jit(solution)/shard_map/cond/branch_1_fun/dot_general | solution.py:134
  497.1 13.7 %collective-permute-start.2 = (bf16[2,256,1536]{1,2,0:T(8,128)(2,1)}, bf16[2,256,1536]{1,2,0:T(8,128)(2,1)}, u32[]{:S(2)}, u32[]{:S(2)}) collective-permute-start(bf16[2,256,1536]{1,2,0:T(8,128)(2,1)} %pad_maximum_fusion.1), channel_id=1, source_target_pairs={{2,0},{4,2},{6,4},{8,6},{10,8},{12,10},{14,12},{16,14},{18,16},{20... | collective-permute-start | bytes 4718600 | tf_op jit(solution)/shard_map/cond/branch_1_fun/ppermute | solution.py:20
  519.4 9.1 %conditional.2 = (f32[12,512]{1,0:T(8,128)S(1)}, f32[12,512]{1,0:T(8,128)S(1)}, f32[512,12,128]{0,2,1:T(8,128)}) conditional(s32[]{:T(128)} %convert_element_type.131, () %tuple.74, (bf16[512,12,128]{0,2,1:T(8,128)(2,1)S(1)}, bf16[256,12,128]{0,2,1:T(8,128)(2,1)S(1)}, bf16[256,1536]{0,1:T(8,128)(2,1)S(1)}) %tuple.338), branch_computations={%region_26.26_spmd, %region_27.29_spmd} | conditional | flops 817876992 | bytes 31752272 | solution.py:116
  521.8 3.1 fusion.26
  524.9 3.7 copy.126
  528.5 67.0 %collective-permute-done.3 = bf16[2,256,1536]{1,2,0:T(8,128)(2,1)} collective-permute-done((bf16[2,256,1536]{1,2,0:T(8,128)(2,1)}, bf16[2,256,1536]{1,2,0:T(8,128)(2,1)}, u32[]{:S(2)}, u32[]{:S(2)}) %collective-permute-start.3) | collective-permute-done | bytes 1572896 | tf_op jit(solution)/shard_map/cond/branch_1_fun/ppermute | solution.py:20
  602.0 4.2 conditional
  606.3 7.0 %divide_convert_fusion = bf16[512,12,128]{0,2,1:T(8,128)(2,1)S(1)} fusion(f32[512,12,128]{0,2,1:T(8,128)} %get-tuple-element.209, f32[512,12,128]{0,2,1:T(8,128)} %get-tuple-element.208, f32[512,12,128]{0,2,1:T(8,128)} %get-tuple-element.207, f32[512,12,128]{0,2,1:T(8,128)} %get-tuple-element.206, f32[512,12,128]{0,2,1:T(8,128)} %get-tuple-element.205, ...), kind=kLoop, calls=%fused_computation.93 | loop fusion | flops 12582912 | bytes 17571840 | tf_op jit(solution)/shard_map/cond/branch_1_fun/convert_element_type | solution.py:72
  613.4 10.7 %fusion.190 = f32[512,3072]{1,0:T(8,128)} fusion(bf16[512,1536]{0,1:T(8,128)(2,1)S(1)} %bitcast.260, bf16[1536,3072]{1,0:T(8,128)(2,1)} %get-tuple-element.127), kind=kOutput, calls=%fused_computation.388 | convolution fusion | flops 4831838208 | bytes 17301504 | tf_op jit(solution)/shard_map/cond/branch_1_fun/dot_general | solution.py:133
  626.6 50.3 %reduce-scatter.3.cloned.1.call-done = f32[512,1536]{1,0:T(8,128)} async-done(((f32[512,3072]{1,0:T(8,128)}), f32[512,1536]{1,0:T(8,128)}) %reduce-scatter.3.cloned.1.call-update) | async-done | bytes 3145744 | tf_op jit(solution)/shard_map/cond/branch_1_fun/reduce_scatter | solution.py:136
  676.9 3.2 convert_element_type.135
  (307 shorter events, 131.6 us)
Async XLA Ops:
  12.4 16.2 %collective-permute-start.8 = (bf16[1536,128]{1,0:T(8,128)(2,1)}, bf16[1536,128]{1,0:T(8,128)(2,1)S(1)}, u32[]{:S(2)}, u32[]{:S(2)}) collective-permute-start(bf16[1536,128]{1,0:T(8,128)(2,1)} %pad_maximum_fusion.5), channel_id=1, source_target_pairs={{0,2},{2,0},{4,6},{6,4},{8,10},{10,8},{12,14},{14,12},{16,18},{18,... | collective-permute-start | bytes 1179656 | tf_op jit(solution)/shard_map/ppermute | solution.py:225
  14.4 17.7 %collective-permute-start.9 = (bf16[1536,128]{1,0:T(8,128)(2,1)}, bf16[1536,128]{1,0:T(8,128)(2,1)S(1)}, u32[]{:S(2)}, u32[]{:S(2)}) collective-permute-start(bf16[1536,128]{1,0:T(8,128)(2,1)} %pad_maximum_fusion.6), channel_id=1, source_target_pairs={{0,4},{2,6},{4,0},{6,2},{8,12},{10,14},{12,8},{14,10},{16,20},{18,... | collective-permute-start | bytes 1179656 | tf_op jit(solution)/shard_map/ppermute | solution.py:225
  15.4 16.7 %collective-permute-start.10 = (bf16[1536,128]{1,0:T(8,128)(2,1)}, bf16[1536,128]{1,0:T(8,128)(2,1)S(1)}, u32[]{:S(2)}, u32[]{:S(2)}) collective-permute-start(bf16[1536,128]{1,0:T(8,128)(2,1)} %pad_maximum_fusion.7), channel_id=1, source_target_pairs={{0,6},{2,4},{4,2},{6,0},{8,14},{10,12},{12,10},{14,8},{16,22},{18,... | collective-permute-start | bytes 1179656 | tf_op jit(solution)/shard_map/ppermute | solution.py:225
  17.4 22.1 %collective-permute-start.15 = (bf16[1536,128]{1,0:T(8,128)(2,1)}, bf16[1536,128]{1,0:T(8,128)(2,1)S(1)}, u32[]{:S(2)}, u32[]{:S(2)}) collective-permute-start(bf16[1536,128]{1,0:T(8,128)(2,1)} %pad_maximum_fusion.9), channel_id=1, source_target_pairs={{0,2},{2,0},{4,6},{6,4},{8,10},{10,8},{12,14},{14,12},{16,18},{18,... | collective-permute-start | bytes 1179656 | tf_op jit(solution)/shard_map/ppermute | solution.py:225
  19.4 29.5 %collective-permute-start.16 = (bf16[1536,128]{1,0:T(8,128)(2,1)}, bf16[1536,128]{1,0:T(8,128)(2,1)S(1)}, u32[]{:S(2)}, u32[]{:S(2)}) collective-permute-start(bf16[1536,128]{1,0:T(8,128)(2,1)} %pad_maximum_fusion.10), channel_id=1, source_target_pairs={{0,4},{2,6},{4,0},{6,2},{8,12},{10,14},{12,8},{14,10},{16,20},{18,... | collective-permute-start | bytes 1179656 | tf_op jit(solution)/shard_map/ppermute | solution.py:225
  28.6 23.4 %collective-permute-start.17 = (bf16[1536,128]{1,0:T(8,128)(2,1)S(1)}, bf16[1536,128]{1,0:T(8,128)(2,1)S(1)}, u32[]{:S(2)}, u32[]{:S(2)}) collective-permute-start(bf16[1536,128]{1,0:T(8,128)(2,1)S(1)} %pad_maximum_fusion.11), channel_id=1, source_target_pairs={{0,6},{2,4},{4,2},{6,0},{8,14},{10,12},{12,10},{14,8},{16,22},{18,... | collective-permute-start | bytes 1179656 | tf_op jit(solution)/shard_map/ppermute | solution.py:225
  32.1 24.3 %collective-permute-start.22 = (bf16[1536,128]{1,0:T(8,128)(2,1)S(1)}, bf16[1536,128]{1,0:T(8,128)(2,1)S(1)}, u32[]{:S(2)}, u32[]{:S(2)}) collective-permute-start(bf16[1536,128]{1,0:T(8,128)(2,1)S(1)} %pad_maximum_fusion.13), channel_id=1, source_target_pairs={{0,2},{2,0},{4,6},{6,4},{8,10},{10,8},{12,14},{14,12},{16,18},{18,... | collective-permute-start | bytes 1179656 | tf_op jit(solution)/shard_map/ppermute | solution.py:225
  32.1 34.3 %collective-permute-start.23 = (bf16[1536,128]{1,0:T(8,128)(2,1)S(1)}, bf16[1536,128]{1,0:T(8,128)(2,1)S(1)}, u32[]{:S(2)}, u32[]{:S(2)}) collective-permute-start(bf16[1536,128]{1,0:T(8,128)(2,1)S(1)} %pad_maximum_fusion.14), channel_id=1, source_target_pairs={{0,4},{2,6},{4,0},{6,2},{8,12},{10,14},{12,8},{14,10},{16,20},{18,... | collective-permute-start | bytes 1179656 | tf_op jit(solution)/shard_map/ppermute | solution.py:225
  39.5 29.0 %collective-permute-start.24 = (bf16[1536,128]{1,0:T(8,128)(2,1)S(1)}, bf16[1536,128]{1,0:T(8,128)(2,1)S(1)}, u32[]{:S(2)}, u32[]{:S(2)}) collective-permute-start(bf16[1536,128]{1,0:T(8,128)(2,1)S(1)} %pad_maximum_fusion.15), channel_id=1, source_target_pairs={{0,6},{2,4},{4,2},{6,0},{8,14},{10,12},{12,10},{14,8},{16,22},{18,... | collective-permute-start | bytes 1179656 | tf_op jit(solution)/shard_map/ppermute | solution.py:225
  48.9 23.1 %collective-permute-start.11 = (bf16[2,512,128]{2,1,0:T(8,128)(2,1)S(1)}, bf16[2,512,128]{2,1,0:T(8,128)(2,1)S(1)}, u32[]{:S(2)}, u32[]{:S(2)}) collective-permute-start(bf16[2,512,128]{2,1,0:T(8,128)(2,1)S(1)} %pad_maximum_fusion.19), channel_id=1, source_target_pairs={{0,8},{2,10},{4,12},{6,14},{8,16},{10,18},{12,20},{14,22},{16,24},... | collective-permute-start | bytes 786440 | tf_op jit(solution)/shard_map/ppermute | solution.py:20
  52.1 22.0 %collective-permute-start.12 = (bf16[2,512,128]{2,1,0:T(8,128)(2,1)S(1)}, bf16[2,512,128]{2,1,0:T(8,128)(2,1)S(1)}, u32[]{:S(2)}, u32[]{:S(2)}) collective-permute-start(bf16[2,512,128]{2,1,0:T(8,128)(2,1)S(1)} %pad_maximum_fusion.20), channel_id=1, source_target_pairs={{8,0},{10,2},{12,4},{14,6},{16,8},{18,10},{20,12},{22,14},{24,16},... | collective-permute-start | bytes 786440 | tf_op jit(solution)/shard_map/ppermute | solution.py:20
  56.4 29.8 %collective-permute-start.18 = (bf16[2,512,128]{2,1,0:T(8,128)(2,1)S(1)}, bf16[2,512,128]{2,1,0:T(8,128)(2,1)S(1)}, u32[]{:S(2)}, u32[]{:S(2)}) collective-permute-start(bf16[2,512,128]{2,1,0:T(8,128)(2,1)S(1)} %pad_maximum_fusion.21), channel_id=1, source_target_pairs={{0,8},{2,10},{4,12},{6,14},{8,16},{10,18},{12,20},{14,22},{16,24},... | collective-permute-start | bytes 786440 | tf_op jit(solution)/shard_map/ppermute | solution.py:20
  66.4 21.7 %collective-permute-start.19 = (bf16[2,512,128]{2,1,0:T(8,128)(2,1)S(1)}, bf16[2,512,128]{2,1,0:T(8,128)(2,1)S(1)}, u32[]{:S(2)}, u32[]{:S(2)}) collective-permute-start(bf16[2,512,128]{2,1,0:T(8,128)(2,1)S(1)} %pad_maximum_fusion.22), channel_id=1, source_target_pairs={{8,0},{10,2},{12,4},{14,6},{16,8},{18,10},{20,12},{22,14},{24,16},... | collective-permute-start | bytes 786440 | tf_op jit(solution)/shard_map/ppermute | solution.py:20
  68.7 31.7 %collective-permute-start.25 = (bf16[2,512,128]{2,1,0:T(8,128)(2,1)S(1)}, bf16[2,512,128]{2,1,0:T(8,128)(2,1)S(1)}, u32[]{:S(2)}, u32[]{:S(2)}) collective-permute-start(bf16[2,512,128]{2,1,0:T(8,128)(2,1)S(1)} %pad_maximum_fusion.23), channel_id=1, source_target_pairs={{0,8},{2,10},{4,12},{6,14},{8,16},{10,18},{12,20},{14,22},{16,24},... | collective-permute-start | bytes 786440 | tf_op jit(solution)/shard_map/ppermute | solution.py:20
  72.0 28.4 %collective-permute-start.26 = (bf16[2,512,128]{2,1,0:T(8,128)(2,1)S(1)}, bf16[2,512,128]{2,1,0:T(8,128)(2,1)S(1)}, u32[]{:S(2)}, u32[]{:S(2)}) collective-permute-start(bf16[2,512,128]{2,1,0:T(8,128)(2,1)S(1)} %pad_maximum_fusion.24), channel_id=1, source_target_pairs={{8,0},{10,2},{12,4},{14,6},{16,8},{18,10},{20,12},{22,14},{24,16},... | collective-permute-start | bytes 786440 | tf_op jit(solution)/shard_map/ppermute | solution.py:20
  80.9 62.3 %collective-permute-start.13 = (bf16[2,256,256]{2,1,0:T(8,128)(2,1)S(1)}, bf16[2,256,256]{2,1,0:T(8,128)(2,1)S(1)}, u32[]{:S(2)}, u32[]{:S(2)}) collective-permute-start(bf16[2,256,256]{2,1,0:T(8,128)(2,1)S(1)} %get-tuple-element.387), channel_id=1, source_target_pairs={{0,8},{2,10},{4,12},{6,14},{8,16},{10,18},{12,20},{14,22},{16,24},... | collective-permute-start | bytes 786440 | tf_op jit(solution)/shard_map/ppermute | solution.py:20
  86.2 60.4 %collective-permute-start.14 = (bf16[2,256,256]{2,1,0:T(8,128)(2,1)S(1)}, bf16[2,256,256]{2,1,0:T(8,128)(2,1)S(1)}, u32[]{:S(2)}, u32[]{:S(2)}) collective-permute-start(bf16[2,256,256]{2,1,0:T(8,128)(2,1)S(1)} %get-tuple-element.386), channel_id=1, source_target_pairs={{8,0},{10,2},{12,4},{14,6},{16,8},{18,10},{20,12},{22,14},{24,16},... | collective-permute-start | bytes 786440 | tf_op jit(solution)/shard_map/ppermute | solution.py:20
  95.0 60.6 %collective-permute-start.20 = (bf16[2,256,256]{2,1,0:T(8,128)(2,1)S(1)}, bf16[2,256,256]{2,1,0:T(8,128)(2,1)S(1)}, u32[]{:S(2)}, u32[]{:S(2)}) collective-permute-start(bf16[2,256,256]{2,1,0:T(8,128)(2,1)S(1)} %get-tuple-element.385), channel_id=1, source_target_pairs={{0,8},{2,10},{4,12},{6,14},{8,16},{10,18},{12,20},{14,22},{16,24},... | collective-permute-start | bytes 786440 | tf_op jit(solution)/shard_map/ppermute | solution.py:20
  107.3 4.9 collective-permute-start.29
  107.4 5.3 collective-permute-start.32
  112.2 4.6 collective-permute-start.35
  112.7 5.1 collective-permute-start.30
  116.8 6.4 collective-permute-start.31
  117.8 5.5 collective-permute-start.33
  123.2 6.0 collective-permute-start.34
  123.3 6.0 collective-permute-start.36
  129.2 4.1 collective-permute-start.37
  129.2 27.0 %collective-permute-start.21 = (bf16[2,256,256]{2,1,0:T(8,128)(2,1)S(1)}, bf16[2,256,256]{2,1,0:T(8,128)(2,1)S(1)}, u32[]{:S(2)}, u32[]{:S(2)}) collective-permute-start(bf16[2,256,256]{2,1,0:T(8,128)(2,1)S(1)} %get-tuple-element.384), channel_id=1, source_target_pairs={{8,0},{10,2},{12,4},{14,6},{16,8},{18,10},{20,12},{22,14},{24,16},... | collective-permute-start | bytes 786440 | tf_op jit(solution)/shard_map/ppermute | solution.py:20
  133.3 25.2 %collective-permute-start.27 = (bf16[2,256,256]{2,1,0:T(8,128)(2,1)S(1)}, bf16[2,256,256]{2,1,0:T(8,128)(2,1)S(1)}, u32[]{:S(2)}, u32[]{:S(2)}) collective-permute-start(bf16[2,256,256]{2,1,0:T(8,128)(2,1)S(1)} %get-tuple-element.383), channel_id=1, source_target_pairs={{0,8},{2,10},{4,12},{6,14},{8,16},{10,18},{12,20},{14,22},{16,24},... | collective-permute-start | bytes 786440 | tf_op jit(solution)/shard_map/ppermute | solution.py:20
  143.2 16.0 %collective-permute-start.28 = (bf16[2,256,256]{2,1,0:T(8,128)(2,1)S(1)}, bf16[2,256,256]{2,1,0:T(8,128)(2,1)S(1)}, u32[]{:S(2)}, u32[]{:S(2)}) collective-permute-start(bf16[2,256,256]{2,1,0:T(8,128)(2,1)S(1)} %get-tuple-element.382), channel_id=1, source_target_pairs={{8,0},{10,2},{12,4},{14,6},{16,8},{18,10},{20,12},{22,14},{24,16},... | collective-permute-start | bytes 786440 | tf_op jit(solution)/shard_map/ppermute | solution.py:20
  146.6 94.5 %collective-permute-start.38 = (f32[512,1536]{1,0:T(8,128)}, f32[512,1536]{1,0:T(8,128)}, u32[]{:S(2)}, u32[]{:S(2)}) collective-permute-start(f32[512,1536]{1,0:T(8,128)} %fusion.138), channel_id=1, source_target_pairs={{0,1},{1,0},{2,3},{3,2},{4,5},{5,4},{6,7},{7,6},{8,9},{9,8},{10,11... | collective-permute-start | bytes 9437192 | tf_op jit(solution)/shard_map/ppermute | solution.py:308
  161.4 5.3 collective-permute-start.39
  162.9 12.3 %collective-permute-start.40 = (bf16[256,128]{1,0:T(8,128)(2,1)S(1)}, bf16[256,128]{1,0:T(8,128)(2,1)S(1)}, u32[]{:S(2)}, u32[]{:S(2)}) collective-permute-start(bf16[256,128]{1,0:T(8,128)(2,1)S(1)} %get-tuple-element.402), channel_id=1, source_target_pairs={{0,6},{2,4},{4,2},{6,0},{8,14},{10,12},{12,10},{14,8},{16,22},{18,... | collective-permute-start | bytes 196616 | tf_op jit(solution)/shard_map/ppermute | solution.py:225
  164.4 11.1 %collective-permute-start.41 = (bf16[256,128]{1,0:T(8,128)(2,1)S(1)}, bf16[256,128]{1,0:T(8,128)(2,1)S(1)}, u32[]{:S(2)}, u32[]{:S(2)}) collective-permute-start(bf16[256,128]{1,0:T(8,128)(2,1)S(1)} %get-tuple-element.400), channel_id=1, source_target_pairs={{0,6},{2,4},{4,2},{6,0},{8,14},{10,12},{12,10},{14,8},{16,22},{18,... | collective-permute-start | bytes 196616 | tf_op jit(solution)/shard_map/ppermute | solution.py:225
  165.2 4.6 collective-permute-start.42
  166.7 10.2 %collective-permute-start.43 = (bf16[256,128]{1,0:T(8,128)(2,1)S(1)}, bf16[256,128]{1,0:T(8,128)(2,1)S(1)}, u32[]{:S(2)}, u32[]{:S(2)}) collective-permute-start(bf16[256,128]{1,0:T(8,128)(2,1)S(1)} %get-tuple-element.408), channel_id=1, source_target_pairs={{0,4},{2,6},{4,0},{6,2},{8,12},{10,14},{12,8},{14,10},{16,20},{18,... | collective-permute-start | bytes 196616 | tf_op jit(solution)/shard_map/ppermute | solution.py:225
  169.9 3.9 collective-permute-start.45
  182.3 53.3 %collective-permute-start.48 = (f32[256,1536]{1,0:T(8,128)}, f32[256,1536]{1,0:T(8,128)}, u32[]{:S(2)}, u32[]{:S(2)}) collective-permute-start(f32[256,1536]{1,0:T(8,128)} %fusion.134), channel_id=1, source_target_pairs={{0,1},{1,0},{2,3},{3,2},{4,5},{5,4},{6,7},{7,6},{8,9},{9,8},{10,11... | collective-permute-start | bytes 4718600 | tf_op jit(solution)/shard_map/ppermute | solution.py:308
  247.7 376.5 %reduce-scatter.5.cloned.1.call-start = ((), (), s32[]{:S(2)}) async-start(), calls=%async_computation.3 | async-start | bytes 4718592 | tf_op jit(solution)/shard_map/cond/branch_1_fun/reduce_scatter | solution.py:137
  252.2 204.3 %collective-permute-start.7 = (bf16[2,512,1536]{1,2,0:T(8,128)(2,1)}, bf16[2,512,1536]{1,2,0:T(8,128)(2,1)}, u32[]{:S(2)}, u32[]{:S(2)}) collective-permute-start(bf16[2,512,1536]{1,2,0:T(8,128)(2,1)} %pad_maximum_fusion), channel_id=1, source_target_pairs={{0,4},{2,6},{4,8},{6,10},{8,12},{10,14},{12,16},{14,18},{16,20},{1... | collective-permute-start | bytes 9437192 | tf_op jit(solution)/shard_map/cond/branch_1_fun/ppermute | solution.py:20
  255.0 202.8 %collective-permute-start.6 = (bf16[2,512,1536]{1,2,0:T(8,128)(2,1)}, bf16[2,512,1536]{1,2,0:T(8,128)(2,1)}, u32[]{:S(2)}, u32[]{:S(2)}) collective-permute-start(bf16[2,512,1536]{1,2,0:T(8,128)(2,1)} %pad_maximum_fusion), channel_id=1, source_target_pairs={{0,2},{2,4},{4,6},{6,8},{8,10},{10,12},{12,14},{14,16},{16,18},{18... | collective-permute-start | bytes 9437192 | tf_op jit(solution)/shard_map/cond/branch_1_fun/ppermute | solution.py:20
  258.3 201.3 %collective-permute-start.5 = (bf16[2,512,1536]{1,2,0:T(8,128)(2,1)}, bf16[2,512,1536]{1,2,0:T(8,128)(2,1)}, u32[]{:S(2)}, u32[]{:S(2)}) collective-permute-start(bf16[2,512,1536]{1,2,0:T(8,128)(2,1)} %pad_maximum_fusion), channel_id=1, source_target_pairs={{2,0},{4,2},{6,4},{8,6},{10,8},{12,10},{14,12},{16,14},{18,16},{20... | collective-permute-start | bytes 9437192 | tf_op jit(solution)/shard_map/cond/branch_1_fun/ppermute | solution.py:20
  261.2 208.3 %collective-permute-start.4 = (bf16[2,512,1536]{1,2,0:T(8,128)(2,1)}, bf16[2,512,1536]{1,2,0:T(8,128)(2,1)}, u32[]{:S(2)}, u32[]{:S(2)}) collective-permute-start(bf16[2,512,1536]{1,2,0:T(8,128)(2,1)} %pad_maximum_fusion), channel_id=1, source_target_pairs={{4,0},{6,2},{8,4},{10,6},{12,8},{14,10},{16,12},{18,14},{20,16},{2... | collective-permute-start | bytes 9437192 | tf_op jit(solution)/shard_map/cond/branch_1_fun/ppermute | solution.py:20
  492.4 184.5 %reduce-scatter.3.cloned.1.call-start = ((), (), s32[]{:S(2)}) async-start(), calls=%async_computation.2 | async-start | bytes 9437184 | tf_op jit(solution)/shard_map/cond/branch_1_fun/reduce_scatter | solution.py:136
  495.2 100.3 %collective-permute-start.3 = (bf16[2,256,1536]{1,2,0:T(8,128)(2,1)}, bf16[2,256,1536]{1,2,0:T(8,128)(2,1)}, u32[]{:S(2)}, u32[]{:S(2)}) collective-permute-start(bf16[2,256,1536]{1,2,0:T(8,128)(2,1)} %pad_maximum_fusion.1), channel_id=1, source_target_pairs={{4,0},{6,2},{8,4},{10,6},{12,8},{14,10},{16,12},{18,14},{20,16},{2... | collective-permute-start | bytes 4718600 | tf_op jit(solution)/shard_map/cond/branch_1_fun/ppermute | solution.py:20
  497.1 100.5 %collective-permute-start.2 = (bf16[2,256,1536]{1,2,0:T(8,128)(2,1)}, bf16[2,256,1536]{1,2,0:T(8,128)(2,1)}, u32[]{:S(2)}, u32[]{:S(2)}) collective-permute-start(bf16[2,256,1536]{1,2,0:T(8,128)(2,1)} %pad_maximum_fusion.1), channel_id=1, source_target_pairs={{2,0},{4,2},{6,4},{8,6},{10,8},{12,10},{14,12},{16,14},{18,16},{20... | collective-permute-start | bytes 4718600 | tf_op jit(solution)/shard_map/cond/branch_1_fun/ppermute | solution.py:20
  510.8 89.0 %collective-permute-start.1 = (bf16[2,256,1536]{1,2,0:T(8,128)(2,1)}, bf16[2,256,1536]{1,2,0:T(8,128)(2,1)}, u32[]{:S(2)}, u32[]{:S(2)}) collective-permute-start(bf16[2,256,1536]{1,2,0:T(8,128)(2,1)} %pad_maximum_fusion.1), channel_id=1, source_target_pairs={{0,2},{2,4},{4,6},{6,8},{8,10},{10,12},{12,14},{14,16},{16,18},{18... | collective-permute-start | bytes 4718600 | tf_op jit(solution)/shard_map/cond/branch_1_fun/ppermute | solution.py:20
  512.7 89.3 %collective-permute-start = (bf16[2,256,1536]{1,2,0:T(8,128)(2,1)}, bf16[2,256,1536]{1,2,0:T(8,128)(2,1)}, u32[]{:S(2)}, u32[]{:S(2)}) collective-permute-start(bf16[2,256,1536]{1,2,0:T(8,128)(2,1)} %pad_maximum_fusion.1), channel_id=1, source_target_pairs={{0,4},{2,6},{4,8},{6,10},{8,12},{10,14},{12,16},{14,18},{16,20},{1... | collective-permute-start | bytes 4718600 | tf_op jit(solution)/shard_map/cond/branch_1_fun/ppermute | solution.py:20
  (50 other events, 434.2 us)
Sparse Core Ops, SparseCore 0:
  492.6 22.2 reduce-scatter.4
  624.3 52.5 reduce-scatter.2

commit v2 on v0

v2 whole, which is shorter than its diff:
```python
import math

import jax
import jax.numpy as jnp
from jax import lax
from jax.experimental import pallas as pl
from jax.experimental.pallas import tpu as pltpu
from jax.sharding import PartitionSpec as P

HEAD_DIM = 128
GROUP = 4
NEG = -1e30
SCALE = 1.0 / math.sqrt(HEAD_DIM)
LOG2E = 1.4426950408889634
LOW, HIGH = 1e-25, 1e25
LOGICAL = pl.DeviceIdType.MESH


def greet(place, base, plane, planes):
    barrier = pltpu.get_barrier_semaphore()
    me = base + place
    for d in range(1, GROUP):
        pl.semaphore_signal(barrier, inc=1, device_id={"seq": base + (place ^ d)}, device_id_type=LOGICAL)

    @pl.when(plane > 0)
    def _():
        pl.semaphore_signal(barrier, inc=1, device_id={"seq": me - GROUP}, device_id_type=LOGICAL)

    @pl.when(plane < planes - 1)
    def _():
        pl.semaphore_signal(barrier, inc=1, device_id={"seq": me + GROUP}, device_id_type=LOGICAL)

    ends = jnp.minimum(plane, 1) + jnp.minimum(planes - 1 - plane, 1)
    pl.semaphore_wait(barrier, GROUP - 1 + ends)


def where_am_i(nblocks):
    me = lax.axis_index("seq")
    place = lax.rem(me, GROUP)
    return me, place, me - place, me // GROUP, nblocks // GROUP


def remote(src, dst, send, recv, target):
    return pltpu.make_async_remote_copy(
        src_ref=src, dst_ref=dst, send_sem=send, recv_sem=recv, device_id={"seq": target}, device_id_type=LOGICAL
    )


def gather_kernel(nblocks, width, k, av, q, vv, k_out, av_out, q_out, vv_out, send, recv, local, zsend, zrecv):
    me, place, base, plane, planes = where_am_i(nblocks)
    greet(place, base, plane, planes)
    pairs = ((k, k_out), (av, av_out), (q, q_out), (vv, vv_out))
    copies = {}
    for n, (src, dst) in enumerate(pairs):
        for d in (3, 1, 2):
            peer = place ^ d
            copies[n, d] = remote(
                src.at[:, pl.ds(pl.multiple_of(peer * width, width), width)],
                dst.at[place],
                send.at[n, d],
                recv.at[n, d],
                base + peer,
            )
            copies[n, d].start()
    own = []
    for n, (src, dst) in enumerate(pairs):
        copy = pltpu.make_async_copy(
            src.at[:, pl.ds(pl.multiple_of(place * width, width), width)], dst.at[place], local.at[n]
        )
        copy.start()
        own.append(copy)
    for n in range(2):
        own[n].wait()
        for d in range(1, GROUP):
            copies[n, d].wait_recv()
    up = [
        remote(x.at[pl.ds(2, 2)], x.at[pl.ds(GROUP, 2)], zsend.at[0, n], zrecv.at[0, n], me + GROUP)
        for n, x in enumerate((k_out, av_out))
    ]
    down = [
        remote(x.at[pl.ds(0, 2)], x.at[pl.ds(GROUP + 2, 2)], zsend.at[1, n], zrecv.at[1, n], me - GROUP)
        for n, x in enumerate((k_out, av_out))
    ]

    @pl.when(plane < planes - 1)
    def _():
        for copy in up:
            copy.start()

    @pl.when(plane > 0)
    def _():
        for copy in down:
            copy.start()

    for n in range(2, 4):
        own[n].wait()
        for d in range(1, GROUP):
            copies[n, d].wait_recv()
    for copy in copies.values():
        copy.wait_send()

    @pl.when(plane < planes - 1)
    def _():
        for copy in up:
            copy.wait_send()
        for copy in down:
            copy.wait_recv()

    @pl.when(plane > 0)
    def _():
        for copy in down:
            copy.wait_send()
        for copy in up:
            copy.wait_recv()


def gather(k, av, q, vv, nblocks):
    vid, aud = q.shape[0], k.shape[0]
    width = q.shape[1] // GROUP
    anyspace = pl.BlockSpec(memory_space=pl.ANY)
    return pl.pallas_call(
        lambda *refs: gather_kernel(nblocks, width, *refs),
        in_specs=[anyspace] * 4,
        out_specs=[anyspace] * 4,
        out_shape=[
            jax.ShapeDtypeStruct((2 * GROUP, aud, width), jnp.bfloat16),
            jax.ShapeDtypeStruct((2 * GROUP, aud, width), jnp.bfloat16),
            jax.ShapeDtypeStruct((GROUP, vid, width), jnp.bfloat16),
            jax.ShapeDtypeStruct((GROUP, vid, width), jnp.bfloat16),
        ],
        scratch_shapes=[
            pltpu.SemaphoreType.DMA((4, GROUP)),
            pltpu.SemaphoreType.DMA((4, GROUP)),
            pltpu.SemaphoreType.DMA((4,)),
            pltpu.SemaphoreType.DMA((2, 2)),
            pltpu.SemaphoreType.DMA((2, 2)),
        ],
        compiler_params=pltpu.CompilerParams(collective_id=0, has_side_effects=True),
    )(k, av, q, vv)


def pair_kernel(valid, k, av, q, vv, o_ref, u_ref, halo_ref, log_ref, avx, vvx, o_acc, u_acc, row_top, col_top):
    vid = q.shape[1]
    aud = k.shape[1]
    avx[:, :, :HEAD_DIM] = av[...]
    vvx[:, :, :HEAD_DIM] = vv[...]
    avx[:, :, HEAD_DIM:] = jnp.ones((2 * GROUP, aud, HEAD_DIM), jnp.bfloat16)
    vvx[:, :, HEAD_DIM:] = jnp.ones((GROUP, vid, HEAD_DIM), jnp.bfloat16)
    o_acc[...] = jnp.zeros_like(o_acc)
    u_acc[...] = jnp.zeros_like(u_acc)
    row_top[...] = jnp.zeros_like(row_top)
    col_top[...] = jnp.zeros_like(col_top)

    def each_pair(body):
        def step(pair, carry):
            @pl.when(valid[pair] != 0)
            def _():
                body(pair // (2 * GROUP), pair % (2 * GROUP))

            return carry

        lax.fori_loop(0, 2 * GROUP * GROUP, step, 0)

    def dot_t(a, b):
        return lax.dot_general(a, b, (((1,), (1,)), ((), ())), preferred_element_type=jnp.float32)

    def fast(row, col):
        weights = jnp.exp2(dot_t(q[row], k[col]) * (SCALE * LOG2E)).astype(jnp.bfloat16)
        o_acc[row] += jnp.dot(weights, avx[col], preferred_element_type=jnp.float32)
        u_acc[col] += lax.dot_general(
            weights, vvx[row], (((0,), (0,)), ((), ())), preferred_element_type=jnp.float32
        )

    each_pair(fast)

    def outside(total):
        wrong = jnp.where((total >= LOW) & (total <= HIGH), 0.0, 1.0)
        return jnp.max(wrong.reshape(-1, 8, HEAD_DIM), axis=0)

    bad = jnp.zeros((8, HEAD_DIM), jnp.float32)
    for slot in range(GROUP):
        bad = jnp.maximum(bad, outside(o_acc[slot, :, HEAD_DIM:]))
    for slot in range(2 * GROUP):
        used = valid[slot]
        for row in range(1, GROUP):
            used = jnp.maximum(used, valid[row * 2 * GROUP + slot])
        bad = jnp.maximum(bad, outside(u_acc[slot, :, HEAD_DIM:]) * used.astype(jnp.float32))

    @pl.when(jnp.max(bad) > 0)
    def _():
        o_acc[...] = jnp.zeros_like(o_acc)
        u_acc[...] = jnp.zeros_like(u_acc)
        row_top[...] = jnp.full_like(row_top, NEG)
        col_top[...] = jnp.full_like(col_top, NEG)

        def update(acc, top, at, scores, values):
            old = top[at]
            new = jnp.maximum(old, jnp.max(scores, axis=1, keepdims=True))
            weights = jnp.exp(scores - new[:, :1]).astype(jnp.bfloat16)
            shrink = jnp.exp(old[:, :1] - new[:, :1])
            top[at] = new
            acc[at] = acc[at] * shrink + jnp.dot(weights, values, preferred_element_type=jnp.float32)

        def safe(row, col):
            update(o_acc, row_top, row, dot_t(q[row], k[col]) * SCALE, avx[col])
            update(u_acc, col_top, col, dot_t(k[col], q[row]) * SCALE, vvx[row])

        each_pair(safe)

    for slot in range(GROUP):
        o_ref[slot] = (o_acc[slot, :, :HEAD_DIM] / o_acc[slot, :, HEAD_DIM:]).astype(jnp.bfloat16)
    for slot in range(2 * GROUP):
        total = u_acc[slot, :, HEAD_DIM:]
        some = total > 0
        mean = jnp.where(some, u_acc[slot, :, :HEAD_DIM] / jnp.where(some, total, 1.0), 0.0)
        logs = jnp.where(some, col_top[slot] + jnp.log(jnp.where(some, total, 1.0)), NEG)
        if slot < GROUP:
            u_ref[slot] = mean
        else:
            halo_ref[slot - GROUP] = mean.astype(jnp.bfloat16)
        log_ref[slot, 0] = jnp.transpose(logs)[:8]


def pair_call(valid, k, av, q, vv):
    vid, aud, width = q.shape[1], k.shape[1], q.shape[2]
    heads = width // HEAD_DIM
    wide = 2 * HEAD_DIM

    def block(*shape):
        return pl.BlockSpec(shape + (HEAD_DIM,), lambda h: (0, 0, h))

    return pl.pallas_call(
        pair_kernel,
        grid=(heads,),
        in_specs=[
            pl.BlockSpec(memory_space=pltpu.SMEM),
            block(2 * GROUP, aud),
            block(2 * GROUP, aud),
            block(GROUP, vid),
            block(GROUP, vid),
        ],
        out_specs=[
            block(GROUP, vid),
            block(GROUP, aud),
            block(GROUP, aud),
            pl.BlockSpec((2 * GROUP, 1, 8, aud), lambda h: (0, h, 0, 0)),
        ],
        out_shape=[
            jax.ShapeDtypeStruct((GROUP, vid, width), jnp.bfloat16),
            jax.ShapeDtypeStruct((GROUP, aud, width), jnp.float32),
            jax.ShapeDtypeStruct((GROUP, aud, width), jnp.bfloat16),
            jax.ShapeDtypeStruct((2 * GROUP, heads, 8, aud), jnp.float32),
        ],
        scratch_shapes=[
            pltpu.VMEM((2 * GROUP, aud, wide), jnp.bfloat16),
            pltpu.VMEM((GROUP, vid, wide), jnp.bfloat16),
            pltpu.VMEM((GROUP, vid, wide), jnp.float32),
            pltpu.VMEM((2 * GROUP, aud, wide), jnp.float32),
            pltpu.VMEM((GROUP, vid, HEAD_DIM), jnp.float32),
            pltpu.VMEM((2 * GROUP, aud, HEAD_DIM), jnp.float32),
        ],
        compiler_params=pltpu.CompilerParams(vmem_limit_bytes=48 * 1024 * 1024),
    )(valid, k, av, q, vv)


def back_kernel(
    nblocks, width, o, u, halo, logs, o_out, u_out, done, got, got_log, send, recv, local, zsend, zrecv
):
    me, place, base, plane, planes = where_am_i(nblocks)
    heads = width // HEAD_DIM
    greet(place, base, plane, planes)
    up = [
        remote(halo.at[pl.ds(2, 2)], got.at[pl.ds(0, 2)], zsend.at[0, 0], zrecv.at[0, 0], me + GROUP),
        remote(logs.at[pl.ds(GROUP + 2, 2)], got_log.at[pl.ds(0, 2)], zsend.at[0, 1], zrecv.at[0, 1], me + GROUP),
    ]
    down = [
        remote(halo.at[pl.ds(0, 2)], got.at[pl.ds(2, 2)], zsend.at[1, 0], zrecv.at[1, 0], me - GROUP),
        remote(logs.at[pl.ds(GROUP, 2)], got_log.at[pl.ds(2, 2)], zsend.at[1, 1], zrecv.at[1, 1], me - GROUP),
    ]

    @pl.when(plane < planes - 1)
    def _():
        for copy in up:
            copy.start()

    @pl.when(plane > 0)
    def _():
        for copy in down:
            copy.start()

    columns = pl.ds(pl.multiple_of(place * width, width), width)
    copies = {}
    for d in (3, 1, 2):
        peer = place ^ d
        copies[0, d] = remote(o.at[peer], o_out.at[:, columns], send.at[0, d], recv.at[0, d], base + peer)
        copies[0, d].start()
    own = pltpu.make_async_copy(o.at[place], o_out.at[:, columns], local.at[0])
    own.start()

    @pl.when(plane > 0)
    def _():
        for copy in up:
            copy.wait_recv()

    @pl.when(plane == 0)
    def _():
        got[0:2] = jnp.zeros((2,) + got.shape[1:], jnp.bfloat16)
        got_log[0:2] = jnp.full((2,) + got_log.shape[1:], NEG, jnp.float32)

    @pl.when(plane < planes - 1)
    def _():
        for copy in down:
            copy.wait_recv()

    @pl.when(plane == planes - 1)
    def _():
        got[2:4] = jnp.zeros((2,) + got.shape[1:], jnp.bfloat16)
        got_log[2:4] = jnp.full((2,) + got_log.shape[1:], NEG, jnp.float32)

    for slot in range(GROUP):
        for h in range(heads):
            cols = slice(h * HEAD_DIM, (h + 1) * HEAD_DIM)
            first, second = logs[slot, h], got_log[slot, h]
            top = jnp.maximum(first, second)
            a, b = jnp.exp(first - top), jnp.exp(second - top)
            share = a / (a + b)
            share = jnp.transpose(jnp.concatenate([share] * (HEAD_DIM // 8), axis=0))
            there = got[slot, :, cols].astype(jnp.float32)
            done[slot, :, cols] = (there + share * (u[slot, :, cols] - there)).astype(jnp.bfloat16)
    for d in (3, 1, 2):
        peer = place ^ d
        copies[1, d] = remote(done.at[peer], u_out.at[:, columns], send.at[1, d], recv.at[1, d], base + peer)
        copies[1, d].start()
    own_u = pltpu.make_async_copy(done.at[place], u_out.at[:, columns], local.at[1])
    own_u.start()
    own.wait()
    own_u.wait()
    for copy in copies.values():
        copy.wait()

    @pl.when(plane < planes - 1)
    def _():
        for copy in up:
            copy.wait_send()

    @pl.when(plane > 0)
    def _():
        for copy in down:
            copy.wait_send()


def give_back(o, u, halo, logs, nblocks):
    vid, aud, width = o.shape[1], u.shape[1], o.shape[2]
    anyspace = pl.BlockSpec(memory_space=pl.ANY)
    vmem = pl.BlockSpec(memory_space=pltpu.VMEM)
    return pl.pallas_call(
        lambda *refs: back_kernel(nblocks, width, *refs),
        in_specs=[anyspace, vmem, vmem, vmem],
        out_specs=[anyspace] * 2,
        out_shape=[
            jax.ShapeDtypeStruct((vid, GROUP * width), jnp.bfloat16),
            jax.ShapeDtypeStruct((aud, GROUP * width), jnp.bfloat16),
        ],
        scratch_shapes=[
            pltpu.VMEM((GROUP, aud, width), jnp.bfloat16),
            pltpu.VMEM((GROUP, aud, width), jnp.bfloat16),
            pltpu.VMEM((GROUP,) + logs.shape[1:], jnp.float32),
            pltpu.SemaphoreType.DMA((2, GROUP)),
            pltpu.SemaphoreType.DMA((2, GROUP)),
            pltpu.SemaphoreType.DMA((2,)),
            pltpu.SemaphoreType.DMA((2, 2)),
            pltpu.SemaphoreType.DMA((2, 2)),
        ],
        compiler_params=pltpu.CompilerParams(
            collective_id=1, has_side_effects=True, vmem_limit_bytes=48 * 1024 * 1024
        ),
    )(o, u, halo, logs)


def shards(
    video_query, video_value, audio_key, audio_value, video_proj, audio_proj, pair_first, pair_count
):
    nblocks = lax.axis_size("seq")
    me = lax.axis_index("seq")
    base = me - me % GROUP
    audio_blocks = base + jnp.asarray(list(range(GROUP)) + [-2, -1, GROUP, GROUP + 1])
    first = lax.dynamic_slice_in_dim(pair_first, base, GROUP)[:, None]
    count = lax.dynamic_slice_in_dim(pair_count, base, GROUP)[:, None]
    valid = (audio_blocks[None, :] >= first) & (audio_blocks[None, :] < first + count)
    valid = valid.astype(jnp.int32).reshape(-1)
    k, av, q, vv = gather(audio_key, audio_value, video_query, video_value, nblocks)
    o, u, halo, logs = pair_call(valid, k, av, q, vv)
    video_attn, audio_attn = give_back(o, u, halo, logs, nblocks)
    half = video_proj.shape[1] // 2
    core = lax.axis_index("head")
    attns = (video_attn, audio_attn)
    projs = (video_proj, audio_proj)

    def part(attn, proj, which):
        columns = lax.dynamic_slice_in_dim(proj, which * half, half, 1)
        return jnp.dot(attn, columns, preferred_element_type=jnp.float32)

    away = [part(a, p, 1 - core) for a, p in zip(attns, projs)]
    arrived = [lax.ppermute(x, "head", [(0, 1), (1, 0)]) for x in away]
    return tuple((part(a, p, core) + x).astype(jnp.bfloat16) for a, p, x in zip(attns, projs, arrived))


def solution(mesh):
    in_specs = (
        P("seq", "head"),
        P("seq", "head"),
        P("seq", "head"),
        P("seq", "head"),
        P("head", None),
        P("head", None),
        P(),
        P(),
    )
    out_specs = (P("seq", "head"), P("seq", "head"))
    return jax.shard_map(shards, mesh=mesh, in_specs=in_specs, out_specs=out_specs, check_vma=False)
```

time: 463 us -> 205 us (0.44)
  waiting for transfers between devices: 261 us -> 5.31 us
  Pallas kernels: 0 us -> 173 us
  local copies, waits for them, and re-layouts: 52.8 us -> 2.64 us
  matrix products: 53.2 us -> 20.9 us
  starting transfers between devices: 32.2 us -> 1.57 us
  other arithmetic: 30.8 us -> 1.48 us
  between operations: 28.4 us -> 0.71 us
    ppermute x8 -> x2, waiting for transfers between devices: 228 us -> 5.31 us  [shards(): arrived = [lax.ppermute(x, 'head', [(0, 1), (1, 0)]) for x in away]]
    pallas_call x0 -> x3, Pallas kernels: none -> 173 us  [the longest x1 75.5 us: pair_call(): pl.pallas_call(pair_kernel, grid=(heads,), in_specs=[pl.BlockSpec(memory_...]
    reduce_scatter x2 -> x0, waiting for transfers between devices: 32.4 us -> none  [the longest x1 32.4 us: shards(): lax.psum_scatter(video_term, 'head', scatter_dimension=1, tiled=True)]
    dot_general x16 -> x4, matrix products: 53.2 us -> 20.9 us  [part(): return jnp.dot(attn, columns, preferred_element_type=jnp.float32)]
    ppermute x8 -> x2, starting transfers between devices: 32.1 us -> 1.57 us  [shards(): arrived = [lax.ppermute(x, 'head', [(0, 1), (1, 0)]) for x in away]]
    cond x39 -> x0, local copies, waits for them, and re-layouts: 26.1 us -> none  [the longest x4 12.2 us: shards(): lax.cond(from_source, audio_side, no_audio, 0)]
    convert_element_type x4 -> x1, other arithmetic: 17.4 us -> 0.07 us  [shards(): valid = valid.astype(jnp.int32).reshape(-1)]
    another operation x12 -> x0, local copies, waits for them, and re-layouts: 10.9 us -> none
  transfers between devices with their start and end apart: 10 -> 2, of which waited for: 3 -> 1; matrix products, arithmetic and copies ran while one was open for 22% -> 4% of each run, Pallas kernels for 0% -> 0%
where the time goes in v2:
time: 205 us; the launch traced here: 206 us
  Pallas kernels  173 us (84%)
  matrix products  20.9 us (10%)
  waiting for transfers between devices  5.31 us (3%)
  local copies, waits for them, and re-layouts  2.64 us (1%)
    pallas_call x1, Pallas kernels, pair_call(): pl.pallas_call(pair_kernel, grid=(heads,), in_specs=[pl.BlockSpec(memory_...  75.5 us
    pallas_call x1, Pallas kernels, gather(): pl.pallas_call(lambda *refs: gather_kernel(nblocks, width, *refs), in_spe...  54.8 us
    pallas_call x1, Pallas kernels, give_back(): pl.pallas_call(lambda *refs: back_kernel(nblocks, width, *refs), in_specs...  42.8 us
    dot_general x4, matrix products, part(): return jnp.dot(attn, columns, preferred_element_type=jnp.float32)  20.9 us
    ppermute x2, waiting for transfers between devices, shards(): arrived = [lax.ppermute(x, 'head', [(0, 1), (1, 0)]) for x in away]  5.31 us
  transfers between devices with their start and end apart: 2, of which 1 were waited for; matrix products, arithmetic and copies ran while one was open for 4% of the time, Pallas kernels for 0%

profile of v2, /device:TPU:13, one launch (start us, length us, event | category | flops | bytes accessed | tf_op | source)
XLA Modules:
  0.0 205.6 jit_solution(10483100297973338620)
XLA Ops:
  0.6 0.7 broadcast_add_fusion
  1.3 0.7 dynamic-slice_add_fusion
  2.1 0.1 and_convert_fusion
  2.1 0.1 reshape.18.valid
  2.2 54.8 %shard_map.104 = (bf16[8,256,384]{2,1,0:T(8,128)(2,1)}, bf16[8,256,384]{2,1,0:T(8,128)(2,1)}, bf16[4,512,384]{2,1,0:T(8,128)(2,1)}, bf16[4,512,384]{2,1,0:T(8,128)(2,1)}) custom-call(bf16[256,1536]{1,0:T(8,128)(2,1)} %refs_0_.1, bf16[256,1536]{1,0:T(8,128)(2,1)} %refs_1_.1, bf16[512,1536]{1,0:T(8,128)(2,1)} %refs_2_.1, bf16[512,1536]{1,0:T(8,128)(2,1)} %refs_3_.1), custom_call_target="tpu_custom_call" | custom-call | tf_op jit(solution)/shard_map/pallas_call | solution.py:121
  57.0 0.0 copy-start.1
  57.0 1.4 copy-done.1
  58.4 75.5 %shard_map.105 = (bf16[4,512,384]{2,1,0:T(8,128)(2,1)S(1)}, f32[4,256,384]{2,1,0:T(8,128)S(1)}, bf16[4,256,384]{2,1,0:T(8,128)(2,1)S(1)}, f32[8,3,8,256]{3,2,1,0:T(8,128)S(1)}) custom-call(s32[32]{0:T(128)S(1)} %reshape.18.valid, bf16[8,256,384]{2,1,0:T(8,128)(2,1)S(1)} %copy-done.1, bf16[8,256,384]{2,1,0:T(8,128)(2,1)} %get-tuple-element.13.av, ...), custom_call_target="tpu_custom_call" | custom-call | tf_op jit(solution)/shard_map/pallas_call | solution.py:232
  133.9 0.0 copy-start
  133.9 1.1 copy-done
  135.0 0.0 slice-start
  135.0 42.8 %shard_map.106 = (bf16[512,1536]{1,0:T(8,128)(2,1)S(1)}, bf16[256,1536]{1,0:T(8,128)(2,1)S(1)}) custom-call(bf16[4,512,384]{2,1,0:T(8,128)(2,1)S(1)} %get-tuple-element.16.refs_0_, f32[4,256,384]{2,1,0:T(8,128)} %copy-done, bf16[4,256,384]{2,1,0:T(8,128)(2,1)S(1)} %get-tuple-element.18.refs_2_, f32[8,3,8,256]{3,2,1,0:T(8,128)S(1)} %get-tuple-element.19.refs_3_), custom_call_target="tpu_custom_call" | custom-call | tf_op jit(solution)/shard_map/pallas_call | solution.py:356
  177.8 0.0 slice-start.1
  177.9 0.0 slice-start.2
  177.9 6.7 %fusion.4 = f32[512,1536]{1,0:T(8,128)} fusion(bf16[512,1536]{1,0:T(8,128)(2,1)S(1)} %get-tuple-element.20, bf16[1536,3072]{1,0:T(8,128)(2,1)} %param.13, s32[]{:T(128)S(6)} %select_n.22), kind=kOutput, calls=%fused_computation.4 | convolution fusion | flops 2415919104 | bytes 9437188 | tf_op jit(solution)/shard_map/dot_general | solution.py:401
  184.6 1.6 collective-permute-start
  186.2 0.0 slice-done
  186.2 0.0 slice-done.1
  186.2 0.0 slice-done.2
  186.2 2.5 %fusion = f32[256,1536]{1,0:T(8,128)} fusion(bf16[256,1536]{1,0:T(8,128)(2,1)S(1)} %get-tuple-element.21, bf16[1536,3072]{1,0:T(8,128)(2,1)S(1)} %bitcast.5, s32[]{:T(128)S(6)} %select_n.22), kind=kOutput, calls=%fused_computation | convolution fusion | flops 1207959552 | bytes 7077892 | tf_op jit(solution)/shard_map/dot_general | solution.py:401
  188.7 0.0 collective-permute-start.1
  188.7 5.3 %collective-permute-done.1 = f32[256,1536]{1,0:T(8,128)} collective-permute-done((f32[256,1536]{1,0:T(8,128)}, f32[256,1536]{1,0:T(8,128)}, u32[]{:S(2)}, u32[]{:S(2)}) %collective-permute-start.1) | collective-permute-done | bytes 1572896 | tf_op jit(solution)/shard_map/ppermute | solution.py:404
  194.0 5.1 %fusion.17 = bf16[256,1536]{1,0:T(8,128)(2,1)} fusion(f32[256,1536]{1,0:T(8,128)} %collective-permute-done.1, bf16[256,1536]{1,0:T(8,128)(2,1)S(1)} %get-tuple-element.21, bf16[1536,3072]{1,0:T(8,128)(2,1)} %param.14, s32[]{:T(128)S(6)} %select_n.21), kind=kOutput, calls=%fused_computation.11 | convolution fusion | flops 1208745984 | bytes 7864324 | tf_op jit(solution)/shard_map/dot_general | solution.py:401
  199.1 0.0 collective-permute-done
  199.1 6.5 %fusion.11 = bf16[512,1536]{1,0:T(8,128)(2,1)} fusion(f32[512,1536]{1,0:T(8,128)} %collective-permute-done, bf16[512,1536]{1,0:T(8,128)(2,1)S(1)} %get-tuple-element.20, bf16[1536,3072]{1,0:T(8,128)(2,1)} %param.13, s32[]{:T(128)S(6)} %select_n.21), kind=kOutput, calls=%fused_computation.9 | convolution fusion | flops 2417491968 | bytes 11010052 | tf_op jit(solution)/shard_map/dot_general | solution.py:401
  (1 shorter events, 0.0 us)
Async XLA Ops:
  57.0 1.4 copy-start.1
  133.9 1.1 copy-start
  135.0 51.1 %slice-start = ((s8[9437184]{0:T(1024)(128)(4,1)}), s8[1048576]{0:T(1024)(128)(4,1)S(1)}, s32[]{:S(2)}) async-start(s8[9437184]{0:T(1024)(128)(4,1)} %bitcast.4), calls=%async_computation | async-start | bytes 2097152
  177.8 8.3 %slice-start.1 = ((s8[9437184]{0:T(1024)(128)(4,1)}), s8[4194304]{0:T(1024)(128)(4,1)S(1)}, s32[]{:S(2)}) async-start(s8[9437184]{0:T(1024)(128)(4,1)} %bitcast.4), calls=%async_computation.1 | async-start | bytes 8388608
  177.9 8.3 %slice-start.2 = ((s8[9437184]{0:T(1024)(128)(4,1)}), s8[4194304]{0:T(1024)(128)(4,1)S(1)}, s32[]{:S(2)}) async-start(s8[9437184]{0:T(1024)(128)(4,1)} %bitcast.4), calls=%async_computation.2 | async-start | bytes 8388608
  184.6 14.5 %collective-permute-start = (f32[512,1536]{1,0:T(8,128)}, f32[512,1536]{1,0:T(8,128)}, u32[]{:S(2)}, u32[]{:S(2)}) collective-permute-start(f32[512,1536]{1,0:T(8,128)} %fusion.4), channel_id=1, source_target_pairs={{0,1},{1,0},{2,3},{3,2},{4,5},{5,4},{6,7},{7,6},{8,9},{9,8},{10,11... | collective-permute-start | bytes 9437192 | tf_op jit(solution)/shard_map/ppermute | solution.py:404
  188.7 5.3 %collective-permute-start.1 = (f32[256,1536]{1,0:T(8,128)}, f32[256,1536]{1,0:T(8,128)}, u32[]{:S(2)}, u32[]{:S(2)}) collective-permute-start(f32[256,1536]{1,0:T(8,128)} %fusion), channel_id=1, source_target_pairs={{0,1},{1,0},{2,3},{3,2},{4,5},{5,4},{6,7},{7,6},{8,9},{9,8},{10,11... | collective-permute-start | bytes 4718600 | tf_op jit(solution)/shard_map/ppermute | solution.py:404

commit v3 on v0

--- a/solution.py
+++ b/solution.py
@@ -3,13 +3,18 @@
 import jax
 import jax.numpy as jnp
 from jax import lax
+from jax.experimental import pallas as pl
+from jax.experimental.pallas import tpu as pltpu
 from jax.sharding import PartitionSpec as P
 
 HEAD_DIM = 128
+GROUP = 4
 HALF = 2
-
-
 NEG = -1e30
+SCALE = 1.0 / math.sqrt(HEAD_DIM)
+LOG2E = 1.4426950408889634
+LOW, HIGH = 1e-25, 1e25
+LOGICAL = pl.DeviceIdType.MESH
 
 
 def shifted(x, axis, by):
@@ -71,7 +76,7 @@
     return result.reshape(result.shape[0], result.shape[1] * result.shape[2])
 
 
-def shards(
+def safe_shards(
     video_query, video_value, audio_key, audio_value, video_proj, audio_proj, pair_first, pair_count
 ):
     heads = video_query.shape[1] // HEAD_DIM
@@ -137,6 +142,459 @@
     return (video_sum.astype(jnp.bfloat16), audio_sum.astype(jnp.bfloat16))
 
 
+def greet(place, base, plane, planes, core):
+    barrier = pltpu.get_barrier_semaphore()
+    for d in range(1, GROUP):
+        pl.semaphore_signal(barrier, inc=1, device_id={"seq": base + (place ^ d)}, device_id_type=LOGICAL)
+    for e in range(1, planes):
+        target = lax.rem(plane + e, planes) * GROUP + place
+        pl.semaphore_signal(barrier, inc=1, device_id={"seq": target}, device_id_type=LOGICAL)
+    pl.semaphore_signal(barrier, inc=1, device_id={"head": 1 - core}, device_id_type=LOGICAL)
+    pl.semaphore_wait(barrier, GROUP + planes - 1)
+
+
+def where_am_i(nblocks):
+    me = lax.axis_index("seq")
+    place = lax.rem(me, GROUP)
+    return me, place, me - place, me // GROUP, nblocks // GROUP
+
+
+def remote(src, dst, send, recv, target):
+    return pltpu.make_async_remote_copy(
+        src_ref=src, dst_ref=dst, send_sem=send, recv_sem=recv, device_id={"seq": target}, device_id_type=LOGICAL
+    )
+
+
+TILE = 512
+SPAN = 2 * HALF + 1
+SLOTS = GROUP + 2 * HALF
+OWN = (4, 5, 0, 1, 2, 3, 6, 7)
+
+
+def dot_t(a, b):
+    return lax.dot_general(a, b, (((1,), (1,)), ((), ())), preferred_element_type=jnp.float32)
+
+
+def write_audio(t, slot, total, summed, top, u_ref, halo_ref, log_ref):
+    some = total > 0
+    mean = jnp.where(some, summed / jnp.where(some, total, 1.0), 0.0)
+    logs = jnp.where(some, top + jnp.log(jnp.where(some, total, 1.0)), NEG)
+    place = OWN[slot]
+    columns = slice(t * HEAD_DIM, (t + 1) * HEAD_DIM)
+    if place < GROUP:
+        u_ref[place, :, columns] = mean
+    else:
+        halo_ref[place - GROUP, :, columns] = mean.astype(jnp.bfloat16)
+    log_ref[place, t] = jnp.transpose(logs)[:8]
+
+
+def whole_kernel(
+    nblocks, heads, bias, used, k, av, q, vv, video_proj, audio_proj,
+    video_out, audio_out, bad_out,
+    k_buf, av_buf, q_buf, vv_buf, o_ref, u_ref, halo_ref, log_ref, bad_ref,
+    avx, vvx, u_acc, video_attn, audio_attn, wide_video, wide_audio,
+    away_video, away_audio, there_video, there_audio, done, got, got_log, flag_out, flag_in,
+    send, recv, local, zsend, zrecv, bsend, brecv, blocal, rsend, rrecv,
+    weight, csend, crecv, fsend, frecv,
+):
+    me, place, base, plane, planes = where_am_i(nblocks)
+    core = lax.axis_index("head")
+    vid, aud = q.shape[0], k.shape[0]
+    greet(place, base, plane, planes, core)
+    arrays = ((k, k_buf, HALF), (av, av_buf, HALF), (q, q_buf, 0), (vv, vv_buf, 0))
+
+    def column(member, t):
+        return pl.ds(pl.multiple_of((member * heads + t) * HEAD_DIM, HEAD_DIM), HEAD_DIM)
+
+    copies, own = {}, {}
+    for t in range(heads):
+        for n, (src, dst, at) in enumerate(arrays):
+            for d in (3, 1, 2):
+                peer = place ^ d
+                copies[t, n, d] = remote(
+                    src.at[:, column(peer, t)], dst.at[t, place + at], send.at[t, n, d], recv.at[t, n, d], base + peer
+                )
+                copies[t, n, d].start()
+    for t in range(heads):
+        for n, (src, dst, at) in enumerate(arrays):
+            own[t, n] = pltpu.make_async_copy(src.at[:, column(place, t)], dst.at[t, place + at], local.at[t, n])
+            own[t, n].start()
+
+    loads = [
+        pltpu.make_async_copy(src, dst, weight.at[n])
+        for n, (src, dst) in enumerate(((video_proj, wide_video), (audio_proj, wide_audio)))
+    ]
+    for load in loads:
+        load.start()
+
+    def returns(t, up):
+        source, target = (HALF, 0) if up else (0, HALF)
+        side = 0 if up else 1
+        columns = slice(t * HEAD_DIM, (t + 1) * HEAD_DIM)
+        pairs = (
+            (halo_ref.at[pl.ds(source, HALF), :, columns], got.at[pl.ds(target, HALF), :, columns]),
+            (log_ref.at[pl.ds(GROUP + source, HALF), t], got_log.at[pl.ds(target, HALF), t]),
+        )
+        return [
+            remote(src, dst, rsend.at[t, side, n], rrecv.at[t, side, n], me + GROUP if up else me - GROUP)
+            for n, (src, dst) in enumerate(pairs)
+        ]
+
+    def backs(n, t):
+        src, dst = ((o_ref, video_attn), (done, audio_attn))[n]
+        columns = slice(t * HEAD_DIM, (t + 1) * HEAD_DIM)
+        return [
+            remote(
+                src.at[place ^ d, :, columns],
+                dst.at[:, column(place, t)],
+                bsend.at[n, t, d],
+                brecv.at[n, t, d],
+                base + (place ^ d),
+            )
+            for d in (3, 1, 2)
+        ], pltpu.make_async_copy(src.at[place, :, columns], dst.at[:, column(place, t)], blocal.at[n, t])
+
+    def start_back(n, t):
+        away, stay = backs(n, t)
+        for copy in away:
+            copy.start()
+        stay.start()
+
+    def wait_back(n):
+        for t in range(heads):
+            away, stay = backs(n, t)
+            for copy in away:
+                copy.wait_recv()
+            stay.wait()
+
+    def finish_audio(t):
+        @pl.when(plane > 0)
+        def _():
+            for copy in returns(t, True):
+                copy.wait_recv()
+
+        @pl.when(plane < planes - 1)
+        def _():
+            for copy in returns(t, False):
+                copy.wait_recv()
+
+        columns = slice(t * HEAD_DIM, (t + 1) * HEAD_DIM)
+        for slot in range(GROUP):
+            first, second = log_ref[slot, t], got_log[slot, t]
+            top = jnp.maximum(first, second)
+            a, b = jnp.exp(first - top), jnp.exp(second - top)
+            share = a / (a + b)
+            share = jnp.transpose(jnp.concatenate([share] * (HEAD_DIM // 8), axis=0))
+            there = got[slot, :, columns].astype(jnp.float32)
+            done[slot, :, columns] = (there + share * (u_ref[slot, :, columns] - there)).astype(jnp.bfloat16)
+        start_back(1, t)
+
+    def relays(t, up):
+        source, target = (GROUP, 0) if up else (HALF, GROUP + HALF)
+        side = 0 if up else 1
+        return [
+            remote(
+                x.at[t, pl.ds(source, HALF)],
+                x.at[t, pl.ds(target, HALF)],
+                zsend.at[t, side, n],
+                zrecv.at[t, side, n],
+                me + GROUP if up else me - GROUP,
+            )
+            for n, x in enumerate((k_buf, av_buf))
+        ]
+
+    avx[:, :, HEAD_DIM:] = jnp.ones((SLOTS, aud, HEAD_DIM), jnp.bfloat16)
+    vvx[:, :, HEAD_DIM:] = jnp.ones((GROUP, vid, HEAD_DIM), jnp.bfloat16)
+
+    @pl.when(plane == 0)
+    def _():
+        for x in (k_buf, av_buf):
+            x[:, :HALF] = jnp.zeros((heads, HALF, aud, HEAD_DIM), jnp.bfloat16)
+
+    @pl.when(plane == planes - 1)
+    def _():
+        for x in (k_buf, av_buf):
+            x[:, GROUP + HALF :] = jnp.zeros((heads, HALF, aud, HEAD_DIM), jnp.bfloat16)
+
+    def outside(total):
+        wrong = jnp.where((total >= LOW) & (total <= HIGH), 0.0, 1.0)
+        return jnp.max(wrong.reshape(-1, 8, HEAD_DIM), axis=0)
+
+    @pl.when(plane == 0)
+    def _():
+        got[:HALF] = jnp.zeros((HALF,) + got.shape[1:], jnp.bfloat16)
+        got_log[:HALF] = jnp.full((HALF,) + got_log.shape[1:], NEG, jnp.float32)
+
+    @pl.when(plane == planes - 1)
+    def _():
+        got[HALF:] = jnp.zeros((HALF,) + got.shape[1:], jnp.bfloat16)
+        got_log[HALF:] = jnp.full((HALF,) + got_log.shape[1:], NEG, jnp.float32)
+
+    bad_ref[...] = jnp.zeros_like(bad_ref)
+    for t in range(heads):
+        for n in range(4):
+            own[t, n].wait()
+            for d in range(1, GROUP):
+                copies[t, n, d].wait_recv()
+            if n == 1:
+
+                @pl.when(plane < planes - 1)
+                def _():
+                    for copy in relays(t, True):
+                        copy.start()
+
+                @pl.when(plane > 0)
+                def _():
+                    for copy in relays(t, False):
+                        copy.start()
+
+        @pl.when(plane < planes - 1)
+        def _():
+            for copy in relays(t, False):
+                copy.wait_recv()
+
+        @pl.when(plane > 0)
+        def _():
+            for copy in relays(t, True):
+                copy.wait_recv()
+
+        avx[:, :, :HEAD_DIM] = av_buf[t]
+        vvx[:, :, :HEAD_DIM] = vv_buf[t]
+        u_acc[...] = jnp.zeros_like(u_acc)
+        columns = slice(t * HEAD_DIM, (t + 1) * HEAD_DIM)
+
+        def step(row, carry):
+            query = q_buf[t, row]
+            weights = jnp.concatenate(
+                [
+                    jnp.exp2(
+                        dot_t(query, k_buf[t, row + c]) * (SCALE * LOG2E) + bias[row * SPAN + c]
+                    ).astype(jnp.bfloat16)
+                    for c in range(SPAN)
+                ],
+                axis=1,
+            )
+            values = avx[pl.ds(row, SPAN)].reshape(SPAN * aud, 2 * HEAD_DIM)
+            out = jnp.dot(weights, values, preferred_element_type=jnp.float32)
+            total = out[:, HEAD_DIM:]
+            o_ref[row, :, columns] = (out[:, :HEAD_DIM] / total).astype(jnp.bfloat16)
+            bad_ref[...] = jnp.maximum(bad_ref[...], outside(total))
+            back = lax.dot_general(
+                weights, vvx[row], (((0,), (0,)), ((), ())), preferred_element_type=jnp.float32
+            )
+            u_acc[pl.ds(row, SPAN)] += back.reshape(SPAN, aud, 2 * HEAD_DIM)
+            return carry
+
+        lax.fori_loop(0, GROUP, step, 0)
+        for slot in range(SLOTS):
+            total = u_acc[slot, :, HEAD_DIM:]
+            bad_ref[...] = jnp.maximum(bad_ref[...], outside(total) * used[slot])
+            write_audio(t, slot, total, u_acc[slot, :, :HEAD_DIM], 0.0, u_ref, halo_ref, log_ref)
+        start_back(0, t)
+
+        @pl.when(plane < planes - 1)
+        def _():
+            for copy in returns(t, True):
+                copy.start()
+
+        @pl.when(plane > 0)
+        def _():
+            for copy in returns(t, False):
+                copy.start()
+
+        if t > 0:
+            finish_audio(t - 1)
+
+    def flags(stage):
+        lines = [{"seq": lax.rem(plane + e, planes) * GROUP + place} for e in range(1, planes)]
+        peers = [{"seq": base + (place ^ d)} for d in range(1, GROUP)]
+        at, targets = ((0, lines), (planes - 1, peers), (planes + GROUP - 2, [{"head": 1 - core}]))[stage]
+        return at, [
+            pltpu.make_async_remote_copy(
+                src_ref=flag_out.at[stage],
+                dst_ref=flag_in.at[at + n],
+                send_sem=fsend.at[at + n],
+                recv_sem=frecv.at[at + n],
+                device_id=target,
+                device_id_type=LOGICAL,
+            )
+            for n, target in enumerate(targets)
+        ]
+
+    def start_flags(stage):
+        flag_out[stage] = bad_ref[...]
+        for copy in flags(stage)[1]:
+            copy.start()
+
+    def end_flags(stage):
+        at, sent = flags(stage)
+        for n, copy in enumerate(sent):
+            copy.wait()
+            bad_ref[...] = jnp.maximum(bad_ref[...], flag_in[at + n])
+
+    start_flags(0)
+    finish_audio(heads - 1)
+    half = video_out.shape[1]
+    tiles = half // TILE
+
+    def columns_of(who, tile):
+        return pl.ds(pl.multiple_of(who * half + tile * TILE, TILE), TILE)
+
+    def project(n, attn, weights, away, there, out):
+        def passing(tile):
+            columns = pl.ds(pl.multiple_of(tile * TILE, TILE), TILE)
+            return pltpu.make_async_remote_copy(
+                src_ref=away.at[:, columns],
+                dst_ref=there.at[:, columns],
+                send_sem=csend.at[n, tile],
+                recv_sem=crecv.at[n, tile],
+                device_id={"head": 1 - core},
+                device_id_type=LOGICAL,
+            )
+
+        def theirs(tile, carry):
+            away[:, pl.ds(pl.multiple_of(tile * TILE, TILE), TILE)] = jnp.dot(
+                attn[...], weights[:, columns_of(1 - core, tile)], preferred_element_type=jnp.float32
+            )
+            passing(tile).start()
+            return carry
+
+        def mine(tile, carry):
+            columns = pl.ds(pl.multiple_of(tile * TILE, TILE), TILE)
+            part = jnp.dot(attn[...], weights[:, columns_of(core, tile)], preferred_element_type=jnp.float32)
+            passing(tile).wait_recv()
+            out[:, columns] = (part + there[:, columns]).astype(jnp.bfloat16)
+            passing(tile).wait_send()
+            return carry
+
+        lax.fori_loop(0, tiles, theirs, 0)
+        lax.fori_loop(0, tiles, mine, 0)
+
+    end_flags(0)
+    start_flags(1)
+    loads[0].wait()
+    wait_back(0)
+    project(0, video_attn, wide_video, away_video, there_video, video_out)
+    end_flags(1)
+    start_flags(2)
+    loads[1].wait()
+    wait_back(1)
+    project(1, audio_attn, wide_audio, away_audio, there_audio, audio_out)
+    end_flags(2)
+    bad_out[...] = bad_ref[...]
+    for copy in copies.values():
+        copy.wait_send()
+    for n in range(2):
+        for t in range(heads):
+            for copy in backs(n, t)[0]:
+                copy.wait_send()
+
+    @pl.when(plane < planes - 1)
+    def _():
+        for t in range(heads):
+            for copy in relays(t, True) + returns(t, True):
+                copy.wait_send()
+
+    @pl.when(plane > 0)
+    def _():
+        for t in range(heads):
+            for copy in relays(t, False) + returns(t, False):
+                copy.wait_send()
+
+
+def whole_call(bias, used, k, av, q, vv, video_proj, audio_proj, nblocks):
+    vid, aud = q.shape[0], k.shape[0]
+    heads = q.shape[1] // HEAD_DIM // GROUP
+    width = heads * HEAD_DIM
+    wide = 2 * HEAD_DIM
+    half = video_proj.shape[1] // 2
+    planes = nblocks // GROUP
+    messages = planes - 1 + GROUP
+    anyspace = pl.BlockSpec(memory_space=pl.ANY)
+    smem = pl.BlockSpec(memory_space=pltpu.SMEM)
+    vmem = pl.BlockSpec(memory_space=pltpu.VMEM)
+    bf16, f32, dma = jnp.bfloat16, jnp.float32, pltpu.SemaphoreType.DMA
+    return pl.pallas_call(
+        lambda *refs: whole_kernel(nblocks, heads, *refs),
+        in_specs=[smem, smem] + [anyspace] * 6,
+        out_specs=[vmem] * 3,
+        out_shape=[
+            jax.ShapeDtypeStruct((vid, half), bf16),
+            jax.ShapeDtypeStruct((aud, half), bf16),
+            jax.ShapeDtypeStruct((8, HEAD_DIM), f32),
+        ],
+        scratch_shapes=[
+            pltpu.VMEM((heads, SLOTS, aud, HEAD_DIM), bf16),
+            pltpu.VMEM((heads, SLOTS, aud, HEAD_DIM), bf16),
+            pltpu.VMEM((heads, GROUP, vid, HEAD_DIM), bf16),
+            pltpu.VMEM((heads, GROUP, vid, HEAD_DIM), bf16),
+            pltpu.VMEM((GROUP, vid, width), bf16),
+            pltpu.VMEM((GROUP, aud, width), f32),
+            pltpu.VMEM((GROUP, aud, width), bf16),
+            pltpu.VMEM((SLOTS, heads, 8, aud), f32),
+            pltpu.VMEM((8, HEAD_DIM), f32),
+            pltpu.VMEM((SLOTS, aud, wide), bf16),
+            pltpu.VMEM((GROUP, vid, wide), bf16),
+            pltpu.VMEM((SLOTS, aud, wide), f32),
+            pltpu.VMEM((vid, GROUP * width), bf16),
+            pltpu.VMEM((aud, GROUP * width), bf16),
+            pltpu.VMEM(video_proj.shape, bf16),
+            pltpu.VMEM(audio_proj.shape, bf16),
+            pltpu.VMEM((vid, half), f32),
+            pltpu.VMEM((aud, half), f32),
+            pltpu.VMEM((vid, half), f32),
+            pltpu.VMEM((aud, half), f32),
+            pltpu.VMEM((GROUP, aud, width), bf16),
+            pltpu.VMEM((GROUP, aud, width), bf16),
+            pltpu.VMEM((GROUP, heads, 8, aud), f32),
+            pltpu.VMEM((3, 8, HEAD_DIM), f32),
+            pltpu.VMEM((messages, 8, HEAD_DIM), f32),
+            dma((heads, 4, GROUP)),
+            dma((heads, 4, GROUP)),
+            dma((heads, 4)),
+            dma((heads, 2, 2)),
+            dma((heads, 2, 2)),
+            dma((2, heads, GROUP)),
+            dma((2, heads, GROUP)),
+            dma((2, heads)),
+            dma((heads, 2, 2)),
+            dma((heads, 2, 2)),
+            dma((2,)),
+            dma((2, half // TILE)),
+            dma((2, half // TILE)),
+            dma((messages,)),
+            dma((messages,)),
+        ],
+        compiler_params=pltpu.CompilerParams(
+            collective_id=0, has_side_effects=True, vmem_limit_bytes=60 * 1024 * 1024
+        ),
+    )(bias, used, k, av, q, vv, video_proj, audio_proj)
+
+
+def shards(
+    video_query, video_value, audio_key, audio_value, video_proj, audio_proj, pair_first, pair_count
+):
+    nblocks = lax.axis_size("seq")
+    me = lax.axis_index("seq")
+    base = me - me % GROUP
+    offsets = jnp.arange(SPAN)[None, :] - HALF + base + jnp.arange(GROUP)[:, None]
+    first = lax.dynamic_slice_in_dim(pair_first, base, GROUP)[:, None]
+    count = lax.dynamic_slice_in_dim(pair_count, base, GROUP)[:, None]
+    valid = (offsets >= first) & (offsets < first + count)
+    bias = jnp.where(valid, 0.0, NEG).astype(jnp.float32).reshape(-1)
+    audio_blocks = base - HALF + jnp.arange(SLOTS)[None, :]
+    used = jnp.any((audio_blocks >= first) & (audio_blocks < first + count), axis=0).astype(jnp.float32)
+    video_out, audio_out, bad = whole_call(
+        bias, used, audio_key, audio_value, video_query, video_value, video_proj, audio_proj, nblocks
+    )
+    arguments = (
+        video_query, video_value, audio_key, audio_value, video_proj, audio_proj, pair_first, pair_count
+    )
+    return lax.cond(
+        jnp.max(bad) > 0, lambda: safe_shards(*arguments), lambda: (video_out, audio_out)
+    )
+
+
 def solution(mesh):
     in_specs = (
         P("seq", "head"),

time: 463 us -> 553 us (1.19); the launches traced: 460 us -> 543 us
  Pallas kernels: 0 us -> 91.9 us
  matrix products: 53.2 us -> 33.9 us
  waiting for transfers between devices: 261 us -> 280 us
  loops' own time: 1.52 us -> 17.8 us
  local copies, waits for them, and re-layouts: 52.8 us -> 37.3 us
  between operations: 28.4 us -> 15.3 us
  starting transfers between devices: 32.2 us -> 39.5 us
    pallas_call x0 -> x1, Pallas kernels: none -> 91.9 us  [whole_call(): pl.pallas_call(lambda *refs: whole_kernel(nblocks, heads, *refs), in_spec...]
    another operation x10 -> x11, loops' own time: 1.52 us -> 17.8 us  [the longest x1 14.2 us: shards(): lax.cond(jnp.max(bad) > 0, lambda: safe_shards(*arguments), lambda: (vide...]
    cond x39 -> x24, local copies, waits for them, and re-layouts: 26.1 us -> 13.1 us  [the longest x3 9.19 us: safe_shards(): lax.cond(from_source, audio_side, no_audio, 0)]
    reduce_scatter x2, waiting for transfers between devices: 32.4 us -> 44.7 us  [the longest x1 44.7 us: safe_shards(): lax.psum_scatter(video_term, 'head', scatter_dimension=1, tiled=True)]
    dot_general x3 -> x1, matrix products: 12.1 us -> 3.14 us  [row_piece(): jnp.einsum('hva,ahe->vhe', expo.astype(jnp.bfloat16), values, preferred_e...]
    ppermute x8, starting transfers between devices: 32.1 us -> 39.4 us  [shifted(): return lax.ppermute(x, axis, pairs)]
    ppermute x8, waiting for transfers between devices: 228 us -> 235 us  [shifted(): return lax.ppermute(x, axis, pairs)]
    dot_general x4 -> x3, matrix products: 13.7 us -> 7.82 us  [col_piece(): jnp.einsum('hva,vhe->ahe', expo.astype(jnp.bfloat16), values, preferred_e...]
  transfers between devices with their start and end apart: 10 -> 10, of which waited for: 3 -> 3; matrix products, arithmetic and copies ran while one was open for 22% -> 12% of each run, Pallas kernels for 0% -> 0%
where the time goes in v3:
time: 553 us; the launch traced here: 543 us
  waiting for transfers between devices  280 us (51%)
  Pallas kernels  91.9 us (17%)
  starting transfers between devices  39.5 us (7%)
  local copies, waits for them, and re-layouts  37.3 us (7%)
  matrix products  33.9 us (6%)
  other arithmetic  27.1 us (5%)
  loops' own time  17.8 us (3%)
  between operations  15.3 us (3%)
    ppermute x8, waiting for transfers between devices, shifted(): return lax.ppermute(x, axis, pairs)  235 us
    pallas_call x1, Pallas kernels, whole_call(): pl.pallas_call(lambda *refs: whole_kernel(nblocks, heads, *refs), in_spec...  91.9 us
    reduce_scatter x1, waiting for transfers between devices, safe_shards(): lax.psum_scatter(video_term, 'head', scatter_dimension=1, tiled=True)  44.7 us
    ppermute x8, starting transfers between devices, shifted(): return lax.ppermute(x, axis, pairs)  39.4 us
    another operation x22, local copies, waits for them, and re-layouts  16.2 us
    another operation x1, loops' own time, shards(): lax.cond(jnp.max(bad) > 0, lambda: safe_shards(*arguments), lambda: (vide...  14.2 us
    convert_element_type x2, other arithmetic, finish(): result = (out / total.T[:, :, None]).astype(jnp.bfloat16)  11.9 us
  transfers between devices with their start and end apart: 10, of which 3 were waited for; matrix products, arithmetic and copies ran while one was open for 12% of the time, Pallas kernels for 0%

profile of v3, /device:TPU:13, one launch (start us, length us, event | category | flops | bytes accessed | tf_op | source)
XLA Modules:
  0.0 542.9 jit_solution(6230818204219518742)
XLA Ops:
  9.2 91.9 %shard_map.99 = (bf16[512,1536]{1,0:T(8,128)(2,1)S(1)}, bf16[256,1536]{1,0:T(8,128)(2,1)}, f32[8,128]{1,0:T(8,128)}) custom-call(f32[20]{0:T(128)} %select_n.22.refs_0_, f32[8]{0:T(128)} %convert_element_type.78.refs_1_, bf16[256,1536]{1,0:T(8,128)(2,1)} %refs_2_.1, bf16[256,1536]{1,0:T(8,128)(2,1)} %refs_3_.1, bf16[512,1536]{1,0:T(8,128)(2,1)} %refs_4_.1, ...), custom_call_target="tpu_custom_call" | custom-call | tf_op jit(solution)/shard_map/pallas_call | solution.py:517
  103.1 429.9 %conditional.11 = ((bf16[512,1536]{1,0:T(8,128)(2,1)S(1)}, bf16[256,1536]{1,0:T(8,128)(2,1)})) conditional(s32[]{:T(128)} %convert_element_type.79, (bf16[512,1536]{1,0:T(8,128)(2,1)S(1)}, bf16[256,1536]{1,0:T(8,128)(2,1)}) %tuple.94, (s32[16]{0:T(128)S(1)}, s32[16]{0:T(128)S(1)}, bf16[512,1536]{1,0:T(8,128)(2,1)S(1)}, bf16[256,1536]{1,0:T(8,128)(2,1)}, ...), branch_computations={%region_2.3_spmd, %region_3.46_spmd} | conditional | flops 15449275392 | bytes 549361472 | solution.py:593
  103.9 1.7 copy.134
  105.6 2.2 pad_maximum_fusion
  107.8 2.8 collective-permute-start.7
  110.6 2.5 collective-permute-start.6
  113.2 3.6 collective-permute-start.5
  116.8 3.4 collective-permute-start.4
  120.2 1.4 copy.132
  132.1 8.4 %conditional.7 = (f32[12,256]{1,0:T(8,128)S(1)}, f32[12,256]{1,0:T(8,128)S(1)}, f32[256,12,128]{0,2,1:T(8,128)}) conditional(s32[]{:T(128)} %convert_element_type.71, () %tuple.84, (bf16[512,1536]{0,1:T(8,128)(2,1)S(1)}, bf16[256,12,128]{0,2,1:T(8,128)(2,1)S(1)}, bf16[512,1536]{0,1:T(8,128)(2,1)}) %tuple.238), branch_computations={%region_33.33_spmd, %region_34.36_spmd} | conditional | flops 817883136 | bytes 33964140 | solution.py:133
  134.8 2.6 fusion.76
  137.4 3.1 copy.190
  140.5 173.4 %collective-permute-done.7 = bf16[2,512,1536]{1,2,0:T(8,128)(2,1)} collective-permute-done((bf16[2,512,1536]{1,2,0:T(8,128)(2,1)}, bf16[2,512,1536]{1,2,0:T(8,128)(2,1)}, u32[]{:S(2)}, u32[]{:S(2)}) %collective-permute-start.7) | collective-permute-done | bytes 3145760 | tf_op jit(solution)/shard_map/cond/branch_1_fun/ppermute | solution.py:23
  313.9 1.3 conditional.9
  315.2 10.3 %conditional.8 = (f32[12,256]{1,0:T(8,128)S(1)}, f32[12,256]{1,0:T(8,128)S(1)}, f32[256,12,128]{0,2,1:T(8,128)}) conditional(s32[]{:T(128)} %convert_element_type.72, () %tuple.86, (bf16[2,512,1536]{1,2,0:T(8,128)(2,1)}, bf16[256,12,128]{0,2,1:T(8,128)(2,1)S(1)}) %tuple.234), branch_computations={%region_37.37_spmd, %region_38.40_spmd} | conditional | flops 817883136 | bytes 33964112 | solution.py:133
  315.6 2.1 fusion.146
  319.8 2.6 fusion.86
  322.4 3.0 copy.192
  325.5 1.4 conditional.6
  325.5 1.3 broadcast.195.clone
  326.8 10.1 %conditional.5 = (f32[12,256]{1,0:T(8,128)S(1)}, f32[12,256]{1,0:T(8,128)S(1)}, f32[256,12,128]{0,2,1:T(8,128)}) conditional(s32[]{:T(128)} %convert_element_type.69, () %tuple.80, (bf16[2,512,1536]{1,2,0:T(8,128)(2,1)}, bf16[256,12,128]{0,2,1:T(8,128)(2,1)S(1)}) %tuple.236), branch_computations={%region_25.25_spmd, %region_26.28_spmd} | conditional | flops 817883136 | bytes 33964112 | solution.py:133
  327.0 2.1 fusion.144
  331.2 2.6 fusion.56
  333.8 3.1 copy.186
  337.0 4.8 divide_convert_fusion.1
  341.8 8.1 %fusion.151 = f32[256,3072]{1,0:T(8,128)} fusion(bf16[256,1536]{0,1:T(8,128)(2,1)S(1)} %bitcast.163, bf16[1536,3072]{1,0:T(8,128)(2,1)} %get-tuple-element.144), kind=kOutput, calls=%fused_computation.172 | convolution fusion | flops 2415919104 | bytes 13369344 | tf_op jit(solution)/shard_map/cond/branch_1_fun/dot_general | solution.py:137
  349.9 1.4 copy.133
  352.6 1.9 collective-permute-start.3
  354.5 21.3 %collective-permute-start.2 = (bf16[2,256,1536]{1,2,0:T(8,128)(2,1)}, bf16[2,256,1536]{1,2,0:T(8,128)(2,1)}, u32[]{:S(2)}, u32[]{:S(2)}) collective-permute-start(bf16[2,256,1536]{1,2,0:T(8,128)(2,1)} %pad_maximum_fusion.1), channel_id=1, source_target_pairs={{2,0},{4,2},{6,4},{8,6},{10,8},{12,10},{14,12},{16,14},{18,16},{20... | collective-permute-start | bytes 4718600 | tf_op jit(solution)/shard_map/cond/branch_1_fun/ppermute | solution.py:23
  375.8 1.9 collective-permute-start.1
  377.7 1.9 collective-permute-start
  383.6 9.0 %conditional.2 = (f32[12,512]{1,0:T(8,128)S(1)}, f32[12,512]{1,0:T(8,128)S(1)}, f32[512,12,128]{0,2,1:T(8,128)}) conditional(s32[]{:T(128)} %convert_element_type.64, () %tuple.74, (bf16[512,12,128]{0,2,1:T(8,128)(2,1)S(1)}, bf16[256,12,128]{0,2,1:T(8,128)(2,1)S(1)}, bf16[256,1536]{0,1:T(8,128)(2,1)S(1)}) %tuple.237), branch_computations={%region_12.12_spmd, %region_13.15_spmd} | conditional | flops 817876992 | bytes 31752272 | solution.py:119
  386.0 3.1 fusion.26
  389.1 3.5 copy.180
  392.6 62.0 %collective-permute-done.3 = bf16[2,256,1536]{1,2,0:T(8,128)(2,1)} collective-permute-done((bf16[2,256,1536]{1,2,0:T(8,128)(2,1)}, bf16[2,256,1536]{1,2,0:T(8,128)(2,1)}, u32[]{:S(2)}, u32[]{:S(2)}) %collective-permute-start.3) | collective-permute-done | bytes 1572896 | tf_op jit(solution)/shard_map/cond/branch_1_fun/ppermute | solution.py:23
  454.7 2.1 conditional.4
  454.7 2.1 broadcast.187.clone
  456.8 2.3 conditional.3
  456.8 2.0 broadcast.183.clone
  459.1 2.1 conditional.1
  459.1 2.1 broadcast.175.clone
  461.2 4.2 conditional
  461.2 2.1 broadcast.171.clone
  465.5 7.2 %divide_convert_fusion = bf16[512,12,128]{0,2,1:T(8,128)(2,1)S(1)} fusion(f32[512,12,128]{0,2,1:T(8,128)} %get-tuple-element.221, f32[512,12,128]{0,2,1:T(8,128)} %get-tuple-element.220, f32[512,12,128]{0,2,1:T(8,128)} %get-tuple-element.219, f32[512,12,128]{0,2,1:T(8,128)} %get-tuple-element.218, f32[512,12,128]{0,2,1:T(8,128)} %get-tuple-element.217, ...), kind=kLoop, calls=%fused_computation.91 | loop fusion | flops 12582912 | bytes 17571840 | tf_op jit(solution)/shard_map/cond/branch_1_fun/convert_element_type | solution.py:75
  472.7 10.7 %fusion.150 = f32[512,3072]{1,0:T(8,128)} fusion(bf16[512,1536]{0,1:T(8,128)(2,1)S(1)} %bitcast.172, bf16[1536,3072]{1,0:T(8,128)(2,1)} %get-tuple-element.127), kind=kOutput, calls=%fused_computation.171 | convolution fusion | flops 4831838208 | bytes 17301504 | tf_op jit(solution)/shard_map/cond/branch_1_fun/dot_general | solution.py:136
  483.5 2.5 convert_element_type.75
  485.9 44.7 %reduce-scatter.3.cloned.1.call-done = f32[512,1536]{1,0:T(8,128)} async-done(((f32[512,3072]{1,0:T(8,128)}), f32[512,1536]{1,0:T(8,128)}) %reduce-scatter.3.cloned.1.call-update) | async-done | bytes 3145744 | tf_op jit(solution)/shard_map/cond/branch_1_fun/reduce_scatter | solution.py:139
  530.6 2.1 convert_element_type.68
  (77 shorter events, 19.0 us)
Async XLA Ops:
  9.2 93.9 %copy-start.2 = (bf16[512,1536]{1,0:T(8,128)(2,1)S(1)}, bf16[512,1536]{1,0:T(8,128)(2,1)}, u32[]{:S(2)}) copy-start(bf16[512,1536]{1,0:T(8,128)(2,1)} %refs_4_.1) | copy-start | bytes 4718596
  9.2 93.9 %copy-start.24 = (s32[16]{0:T(128)S(1)}, s32[16]{0:T(128)}, u32[]{:S(2)}) copy-start(s32[16]{0:T(128)} %param.37) | copy-start | bytes 196
  9.2 93.9 %copy-start.25 = (s32[16]{0:T(128)S(1)}, s32[16]{0:T(128)}, u32[]{:S(2)}) copy-start(s32[16]{0:T(128)} %param.36) | copy-start | bytes 196
  103.1 380.3 %reduce-scatter.5.cloned.1.call-start = ((), (), s32[]{:S(2)}) async-start(), calls=%async_computation.3 | async-start | bytes 4718592 | tf_op jit(solution)/shard_map/cond/branch_1_fun/reduce_scatter | solution.py:140
  105.6 2.2 copy-start
  107.8 206.1 %collective-permute-start.7 = (bf16[2,512,1536]{1,2,0:T(8,128)(2,1)}, bf16[2,512,1536]{1,2,0:T(8,128)(2,1)}, u32[]{:S(2)}, u32[]{:S(2)}) collective-permute-start(bf16[2,512,1536]{1,2,0:T(8,128)(2,1)} %pad_maximum_fusion), channel_id=1, source_target_pairs={{0,4},{2,6},{4,8},{6,10},{8,12},{10,14},{12,16},{14,18},{16,20},{1... | collective-permute-start | bytes 9437192 | tf_op jit(solution)/shard_map/cond/branch_1_fun/ppermute | solution.py:23
  110.6 204.6 %collective-permute-start.6 = (bf16[2,512,1536]{1,2,0:T(8,128)(2,1)}, bf16[2,512,1536]{1,2,0:T(8,128)(2,1)}, u32[]{:S(2)}, u32[]{:S(2)}) collective-permute-start(bf16[2,512,1536]{1,2,0:T(8,128)(2,1)} %pad_maximum_fusion), channel_id=1, source_target_pairs={{0,2},{2,4},{4,6},{6,8},{8,10},{10,12},{12,14},{14,16},{16,18},{18... | collective-permute-start | bytes 9437192 | tf_op jit(solution)/shard_map/cond/branch_1_fun/ppermute | solution.py:23
  113.2 212.3 %collective-permute-start.5 = (bf16[2,512,1536]{1,2,0:T(8,128)(2,1)}, bf16[2,512,1536]{1,2,0:T(8,128)(2,1)}, u32[]{:S(2)}, u32[]{:S(2)}) collective-permute-start(bf16[2,512,1536]{1,2,0:T(8,128)(2,1)} %pad_maximum_fusion), channel_id=1, source_target_pairs={{2,0},{4,2},{6,4},{8,6},{10,8},{12,10},{14,12},{16,14},{18,16},{20... | collective-permute-start | bytes 9437192 | tf_op jit(solution)/shard_map/cond/branch_1_fun/ppermute | solution.py:23
  116.8 210.0 %collective-permute-start.4 = (bf16[2,512,1536]{1,2,0:T(8,128)(2,1)}, bf16[2,512,1536]{1,2,0:T(8,128)(2,1)}, u32[]{:S(2)}, u32[]{:S(2)}) collective-permute-start(bf16[2,512,1536]{1,2,0:T(8,128)(2,1)} %pad_maximum_fusion), channel_id=1, source_target_pairs={{4,0},{6,2},{8,4},{10,6},{12,8},{14,10},{16,12},{18,14},{20,16},{2... | collective-permute-start | bytes 9437192 | tf_op jit(solution)/shard_map/cond/branch_1_fun/ppermute | solution.py:23
  133.4 1.1 copy-start.14
  133.4 1.4 copy-start.1
  137.4 3.1 copy-start.15
  318.7 1.1 copy-start.22
  322.4 3.0 copy-start.23
  330.1 1.1 copy-start.18
  333.8 3.1 copy-start.19
  349.8 180.8 %reduce-scatter.3.cloned.1.call-start = ((), (), s32[]{:S(2)}) async-start(), calls=%async_computation.2 | async-start | bytes 9437184 | tf_op jit(solution)/shard_map/cond/branch_1_fun/reduce_scatter | solution.py:139
  352.6 102.1 %collective-permute-start.3 = (bf16[2,256,1536]{1,2,0:T(8,128)(2,1)}, bf16[2,256,1536]{1,2,0:T(8,128)(2,1)}, u32[]{:S(2)}, u32[]{:S(2)}) collective-permute-start(bf16[2,256,1536]{1,2,0:T(8,128)(2,1)} %pad_maximum_fusion.1), channel_id=1, source_target_pairs={{4,0},{6,2},{8,4},{10,6},{12,8},{14,10},{16,12},{18,14},{20,16},{2... | collective-permute-start | bytes 4718600 | tf_op jit(solution)/shard_map/cond/branch_1_fun/ppermute | solution.py:23
  354.5 102.3 %collective-permute-start.2 = (bf16[2,256,1536]{1,2,0:T(8,128)(2,1)}, bf16[2,256,1536]{1,2,0:T(8,128)(2,1)}, u32[]{:S(2)}, u32[]{:S(2)}) collective-permute-start(bf16[2,256,1536]{1,2,0:T(8,128)(2,1)} %pad_maximum_fusion.1), channel_id=1, source_target_pairs={{2,0},{4,2},{6,4},{8,6},{10,8},{12,10},{14,12},{16,14},{18,16},{20... | collective-permute-start | bytes 4718600 | tf_op jit(solution)/shard_map/cond/branch_1_fun/ppermute | solution.py:23
  375.8 83.3 %collective-permute-start.1 = (bf16[2,256,1536]{1,2,0:T(8,128)(2,1)}, bf16[2,256,1536]{1,2,0:T(8,128)(2,1)}, u32[]{:S(2)}, u32[]{:S(2)}) collective-permute-start(bf16[2,256,1536]{1,2,0:T(8,128)(2,1)} %pad_maximum_fusion.1), channel_id=1, source_target_pairs={{0,2},{2,4},{4,6},{6,8},{8,10},{10,12},{12,14},{14,16},{16,18},{18... | collective-permute-start | bytes 4718600 | tf_op jit(solution)/shard_map/cond/branch_1_fun/ppermute | solution.py:23
  377.7 83.4 %collective-permute-start = (bf16[2,256,1536]{1,2,0:T(8,128)(2,1)}, bf16[2,256,1536]{1,2,0:T(8,128)(2,1)}, u32[]{:S(2)}, u32[]{:S(2)}) collective-permute-start(bf16[2,256,1536]{1,2,0:T(8,128)(2,1)} %pad_maximum_fusion.1), channel_id=1, source_target_pairs={{0,4},{2,6},{4,8},{6,10},{8,12},{10,14},{12,16},{14,18},{16,20},{1... | collective-permute-start | bytes 4718600 | tf_op jit(solution)/shard_map/cond/branch_1_fun/ppermute | solution.py:23
  384.9 1.1 copy-start.3
  389.1 3.5 copy-start.4
  533.0 1.7 copy-start.9
Sparse Core Ops, SparseCore 0:
  350.0 27.6 reduce-scatter.4
  483.6 46.9 reduce-scatter.2

commit v4 on v3

--- a/solution.py
+++ b/solution.py
@@ -135,11 +135,15 @@
     audio_attn = finish(audio_acc)
     video_term = jnp.dot(video_attn, video_proj, preferred_element_type=jnp.float32)
     audio_term = jnp.dot(audio_attn, audio_proj, preferred_element_type=jnp.float32)
-    video_sum, audio_sum = (
-        lax.psum_scatter(video_term, "head", scatter_dimension=1, tiled=True),
-        lax.psum_scatter(audio_term, "head", scatter_dimension=1, tiled=True),
-    )
-    return (video_sum.astype(jnp.bfloat16), audio_sum.astype(jnp.bfloat16))
+    half = video_proj.shape[1] // 2
+    core = lax.axis_index("head")
+
+    def total(term):
+        away = lax.dynamic_slice_in_dim(term, (1 - core) * half, half, 1)
+        mine = lax.dynamic_slice_in_dim(term, core * half, half, 1)
+        return (mine + lax.ppermute(away, "head", [(0, 1), (1, 0)])).astype(jnp.bfloat16)
+
+    return (total(video_term), total(audio_term))
 
 
 def greet(place, base, plane, planes, core):
@@ -206,15 +210,19 @@
     def column(member, t):
         return pl.ds(pl.multiple_of((member * heads + t) * HEAD_DIM, HEAD_DIM), HEAD_DIM)
 
-    copies, own = {}, {}
+    def arrival(t, n, d):
+        src, dst, at = arrays[n]
+        peer = place ^ d
+        return remote(
+            src.at[:, column(peer, t)], dst.at[t, place + at], send.at[t, n, d], recv.at[t, n, d], base + peer
+        )
+
+    own = {}
     for t in range(heads):
-        for n, (src, dst, at) in enumerate(arrays):
-            for d in (3, 1, 2):
-                peer = place ^ d
-                copies[t, n, d] = remote(
-                    src.at[:, column(peer, t)], dst.at[t, place + at], send.at[t, n, d], recv.at[t, n, d], base + peer
-                )
-                copies[t, n, d].start()
+        for group in ((0, 1), (2, 3)):
+            for d in (1, 2, 3):
+                for n in group:
+                    arrival(t, n, d).start()
     for t in range(heads):
         for n, (src, dst, at) in enumerate(arrays):
             own[t, n] = pltpu.make_async_copy(src.at[:, column(place, t)], dst.at[t, place + at], local.at[t, n])
@@ -240,32 +248,30 @@
             for n, (src, dst) in enumerate(pairs)
         ]
 
-    def backs(n, t):
-        src, dst = ((o_ref, video_attn), (done, audio_attn))[n]
-        columns = slice(t * HEAD_DIM, (t + 1) * HEAD_DIM)
-        return [
-            remote(
-                src.at[place ^ d, :, columns],
-                dst.at[:, column(place, t)],
-                bsend.at[n, t, d],
-                brecv.at[n, t, d],
-                base + (place ^ d),
-            )
-            for d in (3, 1, 2)
-        ], pltpu.make_async_copy(src.at[place, :, columns], dst.at[:, column(place, t)], blocal.at[n, t])
-
-    def start_back(n, t):
-        away, stay = backs(n, t)
-        for copy in away:
-            copy.start()
-        stay.start()
+    results = ((o_ref, video_attn), (done, audio_attn))
+
+    def back_copy(n, t, d):
+        src, dst = results[n]
+        peer = place ^ d
+        return remote(
+            src.at[peer, :, pl.ds(t * HEAD_DIM, HEAD_DIM)],
+            dst.at[:, column(place, t)],
+            bsend.at[n, t, d],
+            brecv.at[n, t, d],
+            base + peer,
+        )
+
+    def stay_copy(n, t):
+        src, dst = results[n]
+        return pltpu.make_async_copy(
+            src.at[place, :, pl.ds(t * HEAD_DIM, HEAD_DIM)], dst.at[:, column(place, t)], blocal.at[n, t]
+        )
 
     def wait_back(n):
         for t in range(heads):
-            away, stay = backs(n, t)
-            for copy in away:
-                copy.wait_recv()
-            stay.wait()
+            stay_copy(n, t).wait()
+            for d in range(1, GROUP):
+                back_copy(n, t, d).wait_recv()
 
     def finish_audio(t):
         @pl.when(plane > 0)
@@ -287,7 +293,9 @@
             share = jnp.transpose(jnp.concatenate([share] * (HEAD_DIM // 8), axis=0))
             there = got[slot, :, columns].astype(jnp.float32)
             done[slot, :, columns] = (there + share * (u_ref[slot, :, columns] - there)).astype(jnp.bfloat16)
-        start_back(1, t)
+        stay_copy(1, t).start()
+        for d in (3, 1, 2):
+            back_copy(1, t, d).start()
 
     def relays(t, up):
         source, target = (GROUP, 0) if up else (HALF, GROUP + HALF)
@@ -332,21 +340,20 @@
 
     bad_ref[...] = jnp.zeros_like(bad_ref)
     for t in range(heads):
-        for n in range(4):
+        for n in range(2):
             own[t, n].wait()
             for d in range(1, GROUP):
-                copies[t, n, d].wait_recv()
-            if n == 1:
-
-                @pl.when(plane < planes - 1)
-                def _():
-                    for copy in relays(t, True):
-                        copy.start()
-
-                @pl.when(plane > 0)
-                def _():
-                    for copy in relays(t, False):
-                        copy.start()
+                arrival(t, n, d).wait_recv()
+
+        @pl.when(plane < planes - 1)
+        def _():
+            for copy in relays(t, True):
+                copy.start()
+
+        @pl.when(plane > 0)
+        def _():
+            for copy in relays(t, False):
+                copy.start()
 
         @pl.when(plane < planes - 1)
         def _():
@@ -359,11 +366,23 @@
                 copy.wait_recv()
 
         avx[:, :, :HEAD_DIM] = av_buf[t]
-        vvx[:, :, :HEAD_DIM] = vv_buf[t]
         u_acc[...] = jnp.zeros_like(u_acc)
         columns = slice(t * HEAD_DIM, (t + 1) * HEAD_DIM)
 
-        def step(row, carry):
+        def step(d, carry):
+            row = place ^ d
+
+            @pl.when(d == 0)
+            def _():
+                own[t, 2].wait()
+                own[t, 3].wait()
+
+            @pl.when(d > 0)
+            def _():
+                arrival(t, 2, d).wait_recv()
+                arrival(t, 3, d).wait_recv()
+
+            vvx[row, :, :HEAD_DIM] = vv_buf[t, row]
             query = q_buf[t, row]
             weights = jnp.concatenate(
                 [
@@ -383,6 +402,15 @@
                 weights, vvx[row], (((0,), (0,)), ((), ())), preferred_element_type=jnp.float32
             )
             u_acc[pl.ds(row, SPAN)] += back.reshape(SPAN, aud, 2 * HEAD_DIM)
+
+            @pl.when(d == 0)
+            def _():
+                stay_copy(0, t).start()
+
+            @pl.when(d > 0)
+            def _():
+                back_copy(0, t, d).start()
+
             return carry
 
         lax.fori_loop(0, GROUP, step, 0)
@@ -390,8 +418,6 @@
             total = u_acc[slot, :, HEAD_DIM:]
             bad_ref[...] = jnp.maximum(bad_ref[...], outside(total) * used[slot])
             write_audio(t, slot, total, u_acc[slot, :, :HEAD_DIM], 0.0, u_ref, halo_ref, log_ref)
-        start_back(0, t)
-
         @pl.when(plane < planes - 1)
         def _():
             for copy in returns(t, True):
@@ -481,13 +507,13 @@
     wait_back(1)
     project(1, audio_attn, wide_audio, away_audio, there_audio, audio_out)
     end_flags(2)
-    bad_out[...] = bad_ref[...]
-    for copy in copies.values():
-        copy.wait_send()
-    for n in range(2):
-        for t in range(heads):
-            for copy in backs(n, t)[0]:
-                copy.wait_send()
+    bad_out[0] = jnp.max(bad_ref[...])
+    for t in range(heads):
+        for d in range(1, GROUP):
+            for n in range(4):
+                arrival(t, n, d).wait_send()
+            for n in range(2):
+                back_copy(n, t, d).wait_send()
 
     @pl.when(plane < planes - 1)
     def _():
@@ -517,11 +543,11 @@
     return pl.pallas_call(
         lambda *refs: whole_kernel(nblocks, heads, *refs),
         in_specs=[smem, smem] + [anyspace] * 6,
-        out_specs=[vmem] * 3,
+        out_specs=[vmem, vmem, smem],
         out_shape=[
             jax.ShapeDtypeStruct((vid, half), bf16),
             jax.ShapeDtypeStruct((aud, half), bf16),
-            jax.ShapeDtypeStruct((8, HEAD_DIM), f32),
+            jax.ShapeDtypeStruct((1,), f32),
         ],
         scratch_shapes=[
             pltpu.VMEM((heads, SLOTS, aud, HEAD_DIM), bf16),
@@ -591,7 +617,7 @@
         video_query, video_value, audio_key, audio_value, video_proj, audio_proj, pair_first, pair_count
     )
     return lax.cond(
-        jnp.max(bad) > 0, lambda: safe_shards(*arguments), lambda: (video_out, audio_out)
+        bad[0] > 0, lambda: safe_shards(*arguments), lambda: (video_out, audio_out)
     )
 
 

time: 553 us -> 506 us (0.915)
  waiting for transfers between devices: 280 us -> 232 us
  local copies, waits for them, and re-layouts: 37.3 us -> 51.1 us
  between operations: 15.3 us -> 1.9 us
  starting transfers between devices: 39.5 us -> 31.3 us
    reduce_scatter x2 -> x0, waiting for transfers between devices: 44.7 us -> none  [the longest x1 44.7 us: safe_shards(): lax.psum_scatter(video_term, 'head', scatter_dimension=1, tiled=True)]
    ppermute x8, starting transfers between devices: 39.4 us -> 26.6 us  [shifted(): return lax.ppermute(x, axis, pairs)]
    cond x1 -> x4, local copies, waits for them, and re-layouts: 3.53 us -> 14.4 us  [safe_shards(): video_acc = combine(video_acc, lax.cond(valid, video_side, no_video, 0))]
    dot_general x1 -> x4, matrix products: 3.14 us -> 12.4 us  [row_piece(): jnp.einsum('hva,ahe->vhe', expo.astype(jnp.bfloat16), values, preferred_e...]
    another operation x22 -> x10, local copies, waits for them, and re-layouts: 16.2 us -> 8.2 us
  transfers between devices with their start and end apart: 10 -> 10, of which waited for: 3 -> 3; matrix products, arithmetic and copies ran while one was open for 12% -> 22% of each run, Pallas kernels for 0% -> 0%
where the time goes in v4:
time: 506 us; the launch traced here: 496 us
  waiting for transfers between devices  232 us (46%)
  Pallas kernels  92.2 us (18%)
  local copies, waits for them, and re-layouts  51.1 us (10%)
  matrix products  39.4 us (8%)
  other arithmetic  32.6 us (6%)
  starting transfers between devices  31.3 us (6%)
  loops' own time  15.9 us (3%)
    ppermute x8, waiting for transfers between devices, shifted(): return lax.ppermute(x, axis, pairs)  232 us
    pallas_call x1, Pallas kernels, whole_call(): pl.pallas_call(lambda *refs: whole_kernel(nblocks, heads, *refs), in_spec...  92.2 us
    ppermute x8, starting transfers between devices, shifted(): return lax.ppermute(x, axis, pairs)  26.6 us
    cond x4, local copies, waits for them, and re-layouts, safe_shards(): video_acc = combine(video_acc, lax.cond(valid, video_side, no_video, 0))  14.4 us
    another operation x1, loops' own time, shards(): lax.cond(bad[0] > 0, lambda: safe_shards(*arguments), lambda: (video_out,...  14.2 us
    dot_general x4, matrix products, row_piece(): jnp.einsum('hva,ahe->vhe', expo.astype(jnp.bfloat16), values, preferred_e...  12.4 us
    convert_element_type x2, other arithmetic, finish(): result = (out / total.T[:, :, None]).astype(jnp.bfloat16)  11.9 us
  transfers between devices with their start and end apart: 10, of which 3 were waited for; matrix products, arithmetic and copies ran while one was open for 22% of the time, Pallas kernels for 0%

profile of v4, /device:TPU:13, one launch (start us, length us, event | category | flops | bytes accessed | tf_op | source)
XLA Modules:
  0.0 496.4 jit_solution(16773555620760463735)
XLA Ops:
  2.7 92.2 %shard_map.99 = (bf16[512,1536]{1,0:T(8,128)(2,1)S(1)}, bf16[256,1536]{1,0:T(8,128)(2,1)}, f32[1]{0:T(128)}) custom-call(f32[20]{0:T(128)} %select_n.26.refs_0_, f32[8]{0:T(128)} %convert_element_type.81.refs_1_, bf16[256,1536]{1,0:T(8,128)(2,1)} %refs_2_.1, bf16[256,1536]{1,0:T(8,128)(2,1)} %refs_3_.1, bf16[512,1536]{1,0:T(8,128)(2,1)} %refs_4_.1, ...), custom_call_target="tpu_custom_call" | custom-call | tf_op jit(solution)/shard_map/pallas_call | solution.py:543
  95.5 397.7 %conditional.11 = ((bf16[512,1536]{1,0:T(8,128)(2,1)S(1)}, bf16[256,1536]{1,0:T(8,128)(2,1)})) conditional(s32[]{:T(128)} %bitcast.71, (bf16[512,1536]{1,0:T(8,128)(2,1)S(1)}, bf16[256,1536]{1,0:T(8,128)(2,1)}) %tuple.94, (s32[16]{0:T(128)S(1)}, s32[16]{0:T(128)S(1)}, bf16[512,1536]{1,0:T(8,128)(2,1)}, bf16[256,1536]{1,0:T(8,128)(2,1)S(1)}, ...), branch_computations={%region_1.2_spmd, %region_2.43_spmd} | conditional | flops 15450455040 | bytes 583964672 | solution.py:619
  97.4 3.1 collective-permute-start.3
  100.5 4.9 collective-permute-start.2
  105.4 1.9 collective-permute-start.1
  107.3 3.2 collective-permute-start
  110.5 1.7 copy.131
  112.3 2.6 copy.134
  114.9 3.4 pad_maximum_fusion
  118.2 2.1 collective-permute-start.8
  120.3 148.4 %collective-permute-done.3 = bf16[2,256,1536]{1,2,0:T(8,128)(2,1)} collective-permute-done((bf16[2,256,1536]{1,2,0:T(8,128)(2,1)}, bf16[2,256,1536]{1,2,0:T(8,128)(2,1)}, u32[]{:S(2)}, u32[]{:S(2)}) %collective-permute-start.3) | collective-permute-done | bytes 1572896 | tf_op jit(solution)/shard_map/cond/branch_1_fun/ppermute | solution.py:23
  268.7 4.1 collective-permute-start.7
  272.9 4.1 collective-permute-start.6
  276.9 3.2 collective-permute-start.5
  285.3 8.9 %conditional.2 = (f32[12,512]{1,0:T(8,128)S(1)}, f32[12,512]{1,0:T(8,128)S(1)}, f32[512,12,128]{0,2,1:T(8,128)}) conditional(s32[]{:T(128)} %convert_element_type.66, () %tuple.74, (bf16[512,12,128]{0,2,1:T(8,128)(2,1)S(1)}, bf16[256,12,128]{0,2,1:T(8,128)(2,1)S(1)}, bf16[256,1536]{0,1:T(8,128)(2,1)S(1)}) %tuple.228), branch_computations={%region_11.11_spmd, %region_12.14_spmd} | conditional | flops 817876992 | bytes 31752272 | solution.py:119
  287.5 3.1 fusion.26
  290.6 3.6 copy.180
  294.2 2.0 conditional.4
  294.2 2.0 broadcast.187.clone
  296.3 10.8 %conditional.3 = (f32[12,512]{1,0:T(8,128)S(1)}, f32[12,512]{1,0:T(8,128)S(1)}, f32[512,12,128]{0,2,1:T(8,128)}) conditional(s32[]{:T(128)} %convert_element_type.67, () %tuple.76, (bf16[2,256,1536]{1,2,0:T(8,128)(2,1)}, bf16[512,12,128]{0,2,1:T(8,128)(2,1)S(1)}) %tuple.225), branch_computations={%region_15.15_spmd, %region_16.18_spmd} | conditional | flops 817876992 | bytes 34898000 | solution.py:119
  300.3 3.1 fusion.36
  303.4 3.6 copy.182
  307.0 10.3 %conditional.1 = (f32[12,512]{1,0:T(8,128)S(1)}, f32[12,512]{1,0:T(8,128)S(1)}, f32[512,12,128]{0,2,1:T(8,128)}) conditional(s32[]{:T(128)} %convert_element_type.65, () %tuple.72, (bf16[2,256,1536]{1,2,0:T(8,128)(2,1)}, bf16[512,12,128]{0,2,1:T(8,128)(2,1)S(1)}) %tuple.226), branch_computations={%region_7.7_spmd, %region_8.10_spmd} | conditional | flops 817876992 | bytes 34898000 | solution.py:119
  310.6 3.1 fusion.16
  313.8 3.6 copy.178
  317.3 10.5 %conditional = (f32[12,512]{1,0:T(8,128)S(1)}, f32[12,512]{1,0:T(8,128)S(1)}, f32[512,12,128]{0,2,1:T(8,128)}) conditional(s32[]{:T(128)} %convert_element_type.64, () %tuple.70, (bf16[2,256,1536]{1,2,0:T(8,128)(2,1)}, bf16[512,12,128]{0,2,1:T(8,128)(2,1)S(1)}) %tuple.227), branch_computations={%region_3.3_spmd, %region_4.6_spmd} | conditional | flops 817876992 | bytes 34898000 | solution.py:119
  321.2 3.1 fusion.6
  324.3 3.6 copy.176
  328.0 7.2 %divide_convert_fusion = bf16[512,12,128]{0,2,1:T(8,128)(2,1)S(1)} fusion(f32[512,12,128]{0,2,1:T(8,128)} %get-tuple-element.221, f32[512,12,128]{0,2,1:T(8,128)} %get-tuple-element.220, f32[512,12,128]{0,2,1:T(8,128)} %get-tuple-element.219, f32[512,12,128]{0,2,1:T(8,128)} %get-tuple-element.218, f32[512,12,128]{0,2,1:T(8,128)} %get-tuple-element.217, ...), kind=kLoop, calls=%fused_computation.92 | loop fusion | flops 12582912 | bytes 17571840 | tf_op jit(solution)/shard_map/cond/branch_1_fun/convert_element_type | solution.py:75
  335.1 7.7 %fusion.150 = f32[512,3072]{1,0:T(8,128)S(1)} fusion(bf16[512,1536]{0,1:T(8,128)(2,1)S(1)} %bitcast.173, bf16[1536,3072]{1,0:T(8,128)(2,1)} %get-tuple-element.127), kind=kOutput, calls=%fused_computation.175 | convolution fusion | flops 4831838208 | bytes 17301504 | tf_op jit(solution)/shard_map/cond/branch_1_fun/dot_general | solution.py:136
  342.8 2.2 constant_dynamic-slice_fusion.1
  346.5 2.3 collective-permute-start.4
  358.1 5.9 %conditional.7 = (f32[12,256]{1,0:T(8,128)S(1)}, f32[12,256]{1,0:T(8,128)S(1)}, f32[256,12,128]{0,2,1:T(8,128)}) conditional(s32[]{:T(128)} %convert_element_type.73, () %tuple.84, (bf16[512,1536]{0,1:T(8,128)(2,1)S(1)}, bf16[256,12,128]{0,2,1:T(8,128)(2,1)S(1)}, bf16[512,1536]{0,1:T(8,128)(2,1)}) %tuple.229), branch_computations={%region_31.31_spmd, %region_32.34_spmd} | conditional | flops 817883136 | bytes 33964140 | solution.py:133
  362.3 1.7 copy.190
  364.0 7.3 %conditional.9 = (f32[12,256]{1,0:T(8,128)S(1)}, f32[12,256]{1,0:T(8,128)S(1)}, f32[256,12,128]{0,2,1:T(8,128)}) conditional(s32[]{:T(128)} %convert_element_type.75, () %tuple.88, (bf16[2,512,1536]{1,2,0:T(8,128)(2,1)}, bf16[256,12,128]{0,2,1:T(8,128)(2,1)S(1)}) %tuple.230), branch_computations={%region_39.39_spmd, %region_40.42_spmd} | conditional | flops 817883136 | bytes 33964112 | solution.py:133
  364.0 2.1 fusion.147
  372.9 38.3 %collective-permute-done.6 = bf16[2,512,1536]{1,2,0:T(8,128)(2,1)} collective-permute-done((bf16[2,512,1536]{1,2,0:T(8,128)(2,1)}, bf16[2,512,1536]{1,2,0:T(8,128)(2,1)}, u32[]{:S(2)}, u32[]{:S(2)}) %collective-permute-start.6) | collective-permute-done | bytes 3145760 | tf_op jit(solution)/shard_map/cond/branch_1_fun/ppermute | solution.py:23
  411.2 7.3 %conditional.6 = (f32[12,256]{1,0:T(8,128)S(1)}, f32[12,256]{1,0:T(8,128)S(1)}, f32[256,12,128]{0,2,1:T(8,128)}) conditional(s32[]{:T(128)} %convert_element_type.72, () %tuple.82, (bf16[2,512,1536]{1,2,0:T(8,128)(2,1)}, bf16[256,12,128]{0,2,1:T(8,128)(2,1)S(1)}) %tuple.232), branch_computations={%region_27.27_spmd, %region_28.30_spmd} | conditional | flops 817883136 | bytes 33964112 | solution.py:133
  411.2 2.1 fusion.145
  418.5 45.3 %collective-permute-done.5 = bf16[2,512,1536]{1,2,0:T(8,128)(2,1)} collective-permute-done((bf16[2,512,1536]{1,2,0:T(8,128)(2,1)}, bf16[2,512,1536]{1,2,0:T(8,128)(2,1)}, u32[]{:S(2)}, u32[]{:S(2)}) %collective-permute-start.5) | collective-permute-done | bytes 3145760 | tf_op jit(solution)/shard_map/cond/branch_1_fun/ppermute | solution.py:23
  463.8 7.6 %conditional.5 = (f32[12,256]{1,0:T(8,128)S(1)}, f32[12,256]{1,0:T(8,128)S(1)}, f32[256,12,128]{0,2,1:T(8,128)}) conditional(s32[]{:T(128)} %convert_element_type.71, () %tuple.80, (bf16[2,512,1536]{1,2,0:T(8,128)(2,1)}, bf16[256,12,128]{0,2,1:T(8,128)(2,1)S(1)}) %tuple.233), branch_computations={%region_23.23_spmd, %region_24.26_spmd} | conditional | flops 817883136 | bytes 33964112 | solution.py:133
  464.1 2.1 fusion.144
  471.5 4.8 divide_convert_fusion.1
  476.2 5.2 %fusion.151 = f32[256,3072]{1,0:T(8,128)S(1)} fusion(bf16[256,1536]{0,1:T(8,128)(2,1)S(1)} %bitcast.164, bf16[1536,3072]{1,0:T(8,128)(2,1)} %get-tuple-element.144), kind=kOutput, calls=%fused_computation.176 | convolution fusion | flops 2415919104 | bytes 13369344 | tf_op jit(solution)/shard_map/cond/branch_1_fun/dot_general | solution.py:137
  481.4 1.7 copy-done.1
  484.4 2.3 collective-permute-start.9
  486.7 3.4 add_convert_fusion
  490.5 2.5 add_convert_fusion.1
  (106 shorter events, 45.6 us)
Async XLA Ops:
  2.7 92.8 %copy-start.4 = (bf16[256,1536]{1,0:T(8,128)(2,1)S(1)}, bf16[256,1536]{1,0:T(8,128)(2,1)}, u32[]{:S(2)}) copy-start(bf16[256,1536]{1,0:T(8,128)(2,1)} %refs_2_.1) | copy-start | bytes 2359300
  2.7 92.8 %copy-start.5 = (bf16[256,1536]{1,0:T(8,128)(2,1)S(1)}, bf16[256,1536]{1,0:T(8,128)(2,1)}, u32[]{:S(2)}) copy-start(bf16[256,1536]{1,0:T(8,128)(2,1)} %refs_3_.1) | copy-start | bytes 2359300
  2.7 92.8 %copy-start.27 = (s32[16]{0:T(128)S(1)}, s32[16]{0:T(128)}, u32[]{:S(2)}) copy-start(s32[16]{0:T(128)} %param.37) | copy-start | bytes 196
  2.7 92.8 %copy-start.28 = (s32[16]{0:T(128)S(1)}, s32[16]{0:T(128)}, u32[]{:S(2)}) copy-start(s32[16]{0:T(128)} %param.36) | copy-start | bytes 196
  97.4 171.4 %collective-permute-start.3 = (bf16[2,256,1536]{1,2,0:T(8,128)(2,1)}, bf16[2,256,1536]{1,2,0:T(8,128)(2,1)}, u32[]{:S(2)}, u32[]{:S(2)}) collective-permute-start(bf16[2,256,1536]{1,2,0:T(8,128)(2,1)} %pad_maximum_fusion.1), channel_id=1, source_target_pairs={{4,0},{6,2},{8,4},{10,6},{12,8},{14,10},{16,12},{18,14},{20,16},{2... | collective-permute-start | bytes 4718600 | tf_op jit(solution)/shard_map/cond/branch_1_fun/ppermute | solution.py:23
  100.5 172.3 %collective-permute-start.2 = (bf16[2,256,1536]{1,2,0:T(8,128)(2,1)}, bf16[2,256,1536]{1,2,0:T(8,128)(2,1)}, u32[]{:S(2)}, u32[]{:S(2)}) collective-permute-start(bf16[2,256,1536]{1,2,0:T(8,128)(2,1)} %pad_maximum_fusion.1), channel_id=1, source_target_pairs={{2,0},{4,2},{6,4},{8,6},{10,8},{12,10},{14,12},{16,14},{18,16},{20... | collective-permute-start | bytes 4718600 | tf_op jit(solution)/shard_map/cond/branch_1_fun/ppermute | solution.py:23
  105.4 171.5 %collective-permute-start.1 = (bf16[2,256,1536]{1,2,0:T(8,128)(2,1)}, bf16[2,256,1536]{1,2,0:T(8,128)(2,1)}, u32[]{:S(2)}, u32[]{:S(2)}) collective-permute-start(bf16[2,256,1536]{1,2,0:T(8,128)(2,1)} %pad_maximum_fusion.1), channel_id=1, source_target_pairs={{0,2},{2,4},{4,6},{6,8},{8,10},{10,12},{12,14},{14,16},{16,18},{18... | collective-permute-start | bytes 4718600 | tf_op jit(solution)/shard_map/cond/branch_1_fun/ppermute | solution.py:23
  107.3 210.0 %collective-permute-start = (bf16[2,256,1536]{1,2,0:T(8,128)(2,1)}, bf16[2,256,1536]{1,2,0:T(8,128)(2,1)}, u32[]{:S(2)}, u32[]{:S(2)}) collective-permute-start(bf16[2,256,1536]{1,2,0:T(8,128)(2,1)} %pad_maximum_fusion.1), channel_id=1, source_target_pairs={{0,4},{2,6},{4,8},{6,10},{8,12},{10,14},{12,16},{14,18},{16,20},{1... | collective-permute-start | bytes 4718600 | tf_op jit(solution)/shard_map/cond/branch_1_fun/ppermute | solution.py:23
  118.2 245.8 %collective-permute-start.8 = (bf16[2,512,1536]{1,2,0:T(8,128)(2,1)}, bf16[2,512,1536]{1,2,0:T(8,128)(2,1)}, u32[]{:S(2)}, u32[]{:S(2)}) collective-permute-start(bf16[2,512,1536]{1,2,0:T(8,128)(2,1)} %pad_maximum_fusion), channel_id=1, source_target_pairs={{0,4},{2,6},{4,8},{6,10},{8,12},{10,14},{12,16},{14,18},{16,20},{1... | collective-permute-start | bytes 9437192 | tf_op jit(solution)/shard_map/cond/branch_1_fun/ppermute | solution.py:23
  268.7 102.6 %collective-permute-start.7 = (bf16[2,512,1536]{1,2,0:T(8,128)(2,1)}, bf16[2,512,1536]{1,2,0:T(8,128)(2,1)}, u32[]{:S(2)}, u32[]{:S(2)}) collective-permute-start(bf16[2,512,1536]{1,2,0:T(8,128)(2,1)} %pad_maximum_fusion), channel_id=1, source_target_pairs={{0,2},{2,4},{4,6},{6,8},{8,10},{10,12},{12,14},{14,16},{16,18},{18... | collective-permute-start | bytes 9437192 | tf_op jit(solution)/shard_map/cond/branch_1_fun/ppermute | solution.py:23
  272.9 138.3 %collective-permute-start.6 = (bf16[2,512,1536]{1,2,0:T(8,128)(2,1)}, bf16[2,512,1536]{1,2,0:T(8,128)(2,1)}, u32[]{:S(2)}, u32[]{:S(2)}) collective-permute-start(bf16[2,512,1536]{1,2,0:T(8,128)(2,1)} %pad_maximum_fusion), channel_id=1, source_target_pairs={{2,0},{4,2},{6,4},{8,6},{10,8},{12,10},{14,12},{16,14},{18,16},{20... | collective-permute-start | bytes 9437192 | tf_op jit(solution)/shard_map/cond/branch_1_fun/ppermute | solution.py:23
  276.9 186.9 %collective-permute-start.5 = (bf16[2,512,1536]{1,2,0:T(8,128)(2,1)}, bf16[2,512,1536]{1,2,0:T(8,128)(2,1)}, u32[]{:S(2)}, u32[]{:S(2)}) collective-permute-start(bf16[2,512,1536]{1,2,0:T(8,128)(2,1)} %pad_maximum_fusion), channel_id=1, source_target_pairs={{4,0},{6,2},{8,4},{10,6},{12,8},{14,10},{16,12},{18,14},{20,16},{2... | collective-permute-start | bytes 9437192 | tf_op jit(solution)/shard_map/cond/branch_1_fun/ppermute | solution.py:23
  286.4 1.1 copy-start.6
  290.6 3.6 copy-start.7
  299.2 1.1 copy-start.15
  303.4 3.6 copy-start.16
  309.5 1.1 copy-start.8
  313.8 3.6 copy-start.9
  320.1 1.1 copy-start.10
  324.3 3.6 copy-start.11
  342.8 3.7 copy-start.3
  346.5 140.2 %collective-permute-start.4 = (f32[512,1536]{1,0:T(8,128)}, f32[512,1536]{1,0:T(8,128)}, u32[]{:S(2)}, u32[]{:S(2)}) collective-permute-start(f32[512,1536]{1,0:T(8,128)} %constant_dynamic-slice_fusion.1), channel_id=1, source_target_pairs={{0,1},{1,0},{2,3},{3,2},{4,5},{5,4},{6,7},{7,6},{8,9},{9,8},{10,11... | collective-permute-start | bytes 9437192 | tf_op jit(solution)/shard_map/cond/branch_1_fun/ppermute | solution.py:144
  359.4 1.1 copy-start.17
  359.4 1.4 copy-start
  362.3 1.7 copy-start.18
  367.2 1.1 copy-start.23
  369.7 1.6 copy-start.24
  414.3 1.1 copy-start.19
  416.9 1.6 copy-start.20
  467.2 1.1 copy-start.21
  469.8 1.6 copy-start.22
  481.4 1.7 copy-start.1
  484.4 5.7 %collective-permute-start.9 = (f32[256,1536]{1,0:T(8,128)}, f32[256,1536]{1,0:T(8,128)}, u32[]{:S(2)}, u32[]{:S(2)}) collective-permute-start(f32[256,1536]{1,0:T(8,128)} %constant_dynamic-slice_fusion), channel_id=1, source_target_pairs={{0,1},{1,0},{2,3},{3,2},{4,5},{5,4},{6,7},{7,6},{8,9},{9,8},{10,11... | collective-permute-start | bytes 4718600 | tf_op jit(solution)/shard_map/cond/branch_1_fun/ppermute | solution.py:144
  486.7 3.7 copy-start.2
  493.3 1.7 copy-start.12

commit v5 on v4

--- a/solution.py
+++ b/solution.py
@@ -381,6 +381,9 @@
             def _():
                 arrival(t, 2, d).wait_recv()
                 arrival(t, 3, d).wait_recv()
+                if t == heads - 1:
+                    for e in range(heads - 1):
+                        back_copy(0, e, d).start()
 
             vvx[row, :, :HEAD_DIM] = vv_buf[t, row]
             query = q_buf[t, row]
@@ -407,9 +410,11 @@
             def _():
                 stay_copy(0, t).start()
 
-            @pl.when(d > 0)
-            def _():
-                back_copy(0, t, d).start()
+            if t == heads - 1:
+
+                @pl.when(d > 0)
+                def _():
+                    back_copy(0, t, d).start()
 
             return carry
 
@@ -428,8 +433,9 @@
             for copy in returns(t, False):
                 copy.start()
 
-        if t > 0:
-            finish_audio(t - 1)
+        if t == heads - 1:
+            for e in range(heads - 1):
+                finish_audio(e)
 
     def flags(stage):
         lines = [{"seq": lax.rem(plane + e, planes) * GROUP + place} for e in range(1, planes)]

time: 506 us -> 505 us (level)
  waiting for transfers between devices: 232 us -> 239 us
    ppermute x8, waiting for transfers between devices: 232 us -> 239 us  [shifted(): return lax.ppermute(x, axis, pairs)]
    cond x4 -> x3, local copies, waits for them, and re-layouts: 14.4 us -> 10.8 us  [safe_shards(): video_acc = combine(video_acc, lax.cond(valid, video_side, no_video, 0))]
    dot_general x4 -> x3, matrix products: 12.4 us -> 9.34 us  [row_piece(): jnp.einsum('hva,ahe->vhe', expo.astype(jnp.bfloat16), values, preferred_e...]
    another operation x10 -> x13, local copies, waits for them, and re-layouts: 8.2 us -> 10.3 us
  transfers between devices with their start and end apart: 10 -> 10, of which waited for: 3 -> 3; matrix products, arithmetic and copies ran while one was open for 22% -> 21% of each run, Pallas kernels for 0% -> 0%
where the time goes in v5:
time: 505 us; the launch traced here: 496 us
  waiting for transfers between devices  239 us (47%)
  Pallas kernels  92.8 us (18%)
  local copies, waits for them, and re-layouts  48.1 us (10%)
  matrix products  35.2 us (7%)
  other arithmetic  31.6 us (6%)
  starting transfers between devices  31.4 us (6%)
  loops' own time  15.9 us (3%)
    ppermute x8, waiting for transfers between devices, shifted(): return lax.ppermute(x, axis, pairs)  239 us
    pallas_call x1, Pallas kernels, whole_call(): pl.pallas_call(lambda *refs: whole_kernel(nblocks, heads, *refs), in_spec...  92.8 us
    ppermute x8, starting transfers between devices, shifted(): return lax.ppermute(x, axis, pairs)  26.6 us
    another operation x1, loops' own time, shards(): lax.cond(bad[0] > 0, lambda: safe_shards(*arguments), lambda: (video_out,...  14.2 us
    convert_element_type x2, other arithmetic, finish(): result = (out / total.T[:, :, None]).astype(jnp.bfloat16)  11.9 us
    cond x3, local copies, waits for them, and re-layouts, safe_shards(): video_acc = combine(video_acc, lax.cond(valid, video_side, no_video, 0))  10.8 us
    another operation x13, local copies, waits for them, and re-layouts  10.3 us
  transfers between devices with their start and end apart: 10, of which 3 were waited for; matrix products, arithmetic and copies ran while one was open for 21% of the time, Pallas kernels for 0%

profile of v5, /device:TPU:13, one launch (start us, length us, event | category | flops | bytes accessed | tf_op | source)
XLA Modules:
  0.0 495.8 jit_solution(1990467464418811515)
XLA Ops:
  2.7 92.8 %shard_map.99 = (bf16[512,1536]{1,0:T(8,128)(2,1)S(1)}, bf16[256,1536]{1,0:T(8,128)(2,1)}, f32[1]{0:T(128)}) custom-call(f32[20]{0:T(128)} %select_n.26.refs_0_, f32[8]{0:T(128)} %convert_element_type.81.refs_1_, bf16[256,1536]{1,0:T(8,128)(2,1)} %refs_2_.1, bf16[256,1536]{1,0:T(8,128)(2,1)} %refs_3_.1, bf16[512,1536]{1,0:T(8,128)(2,1)} %refs_4_.1, ...), custom_call_target="tpu_custom_call" | custom-call | tf_op jit(solution)/shard_map/pallas_call | solution.py:549
  96.1 396.6 %conditional.11 = ((bf16[512,1536]{1,0:T(8,128)(2,1)S(1)}, bf16[256,1536]{1,0:T(8,128)(2,1)})) conditional(s32[]{:T(128)} %bitcast.71, (bf16[512,1536]{1,0:T(8,128)(2,1)S(1)}, bf16[256,1536]{1,0:T(8,128)(2,1)}) %tuple.94, (s32[16]{0:T(128)S(1)}, s32[16]{0:T(128)S(1)}, bf16[512,1536]{1,0:T(8,128)(2,1)}, bf16[256,1536]{1,0:T(8,128)(2,1)S(1)}, ...), branch_computations={%region_1.2_spmd, %region_2.43_spmd} | conditional | flops 15450455040 | bytes 583964672 | solution.py:625
  98.0 1.9 collective-permute-start.3
  99.9 5.2 %collective-permute-start.2 = (bf16[2,256,1536]{1,2,0:T(8,128)(2,1)}, bf16[2,256,1536]{1,2,0:T(8,128)(2,1)}, u32[]{:S(2)}, u32[]{:S(2)}) collective-permute-start(bf16[2,256,1536]{1,2,0:T(8,128)(2,1)} %pad_maximum_fusion.1), channel_id=1, source_target_pairs={{2,0},{4,2},{6,4},{8,6},{10,8},{12,10},{14,12},{16,14},{18,16},{20... | collective-permute-start | bytes 4718600 | tf_op jit(solution)/shard_map/cond/branch_1_fun/ppermute | solution.py:23
  105.1 1.9 collective-permute-start.1
  107.0 3.2 collective-permute-start
  110.2 1.7 copy.131
  111.9 2.6 copy.134
  114.5 3.4 pad_maximum_fusion
  117.9 3.1 collective-permute-start.8
  121.0 147.4 %collective-permute-done.3 = bf16[2,256,1536]{1,2,0:T(8,128)(2,1)} collective-permute-done((bf16[2,256,1536]{1,2,0:T(8,128)(2,1)}, bf16[2,256,1536]{1,2,0:T(8,128)(2,1)}, u32[]{:S(2)}, u32[]{:S(2)}) %collective-permute-start.3) | collective-permute-done | bytes 1572896 | tf_op jit(solution)/shard_map/cond/branch_1_fun/ppermute | solution.py:23
  268.3 4.2 collective-permute-start.7
  272.6 4.1 collective-permute-start.6
  276.6 3.2 collective-permute-start.5
  284.9 8.9 %conditional.2 = (f32[12,512]{1,0:T(8,128)S(1)}, f32[12,512]{1,0:T(8,128)S(1)}, f32[512,12,128]{0,2,1:T(8,128)}) conditional(s32[]{:T(128)} %convert_element_type.66, () %tuple.74, (bf16[512,12,128]{0,2,1:T(8,128)(2,1)S(1)}, bf16[256,12,128]{0,2,1:T(8,128)(2,1)S(1)}, bf16[256,1536]{0,1:T(8,128)(2,1)S(1)}) %tuple.228), branch_computations={%region_11.11_spmd, %region_12.14_spmd} | conditional | flops 817876992 | bytes 31752272 | solution.py:119
  287.1 3.1 fusion.26
  290.2 3.6 copy.180
  293.8 2.0 conditional.4
  293.8 2.0 broadcast.187.clone
  295.9 10.8 %conditional.3 = (f32[12,512]{1,0:T(8,128)S(1)}, f32[12,512]{1,0:T(8,128)S(1)}, f32[512,12,128]{0,2,1:T(8,128)}) conditional(s32[]{:T(128)} %convert_element_type.67, () %tuple.76, (bf16[2,256,1536]{1,2,0:T(8,128)(2,1)}, bf16[512,12,128]{0,2,1:T(8,128)(2,1)S(1)}) %tuple.225), branch_computations={%region_15.15_spmd, %region_16.18_spmd} | conditional | flops 817876992 | bytes 34898000 | solution.py:119
  299.9 3.1 fusion.36
  303.0 3.6 copy.182
  306.6 10.3 %conditional.1 = (f32[12,512]{1,0:T(8,128)S(1)}, f32[12,512]{1,0:T(8,128)S(1)}, f32[512,12,128]{0,2,1:T(8,128)}) conditional(s32[]{:T(128)} %convert_element_type.65, () %tuple.72, (bf16[2,256,1536]{1,2,0:T(8,128)(2,1)}, bf16[512,12,128]{0,2,1:T(8,128)(2,1)S(1)}) %tuple.226), branch_computations={%region_7.7_spmd, %region_8.10_spmd} | conditional | flops 817876992 | bytes 34898000 | solution.py:119
  310.3 3.1 fusion.16
  313.4 3.6 copy.178
  317.0 2.3 conditional
  317.0 2.1 broadcast.171.clone
  319.3 7.2 %divide_convert_fusion = bf16[512,12,128]{0,2,1:T(8,128)(2,1)S(1)} fusion(f32[512,12,128]{0,2,1:T(8,128)} %get-tuple-element.221, f32[512,12,128]{0,2,1:T(8,128)} %get-tuple-element.220, f32[512,12,128]{0,2,1:T(8,128)} %get-tuple-element.219, f32[512,12,128]{0,2,1:T(8,128)} %get-tuple-element.218, f32[512,12,128]{0,2,1:T(8,128)} %get-tuple-element.217, ...), kind=kLoop, calls=%fused_computation.92 | loop fusion | flops 12582912 | bytes 17571840 | tf_op jit(solution)/shard_map/cond/branch_1_fun/convert_element_type | solution.py:75
  326.5 7.7 %fusion.150 = f32[512,3072]{1,0:T(8,128)S(1)} fusion(bf16[512,1536]{0,1:T(8,128)(2,1)S(1)} %bitcast.173, bf16[1536,3072]{1,0:T(8,128)(2,1)} %get-tuple-element.127), kind=kOutput, calls=%fused_computation.175 | convolution fusion | flops 4831838208 | bytes 17301504 | tf_op jit(solution)/shard_map/cond/branch_1_fun/dot_general | solution.py:136
  334.2 2.2 constant_dynamic-slice_fusion.1
  337.9 2.1 collective-permute-start.4
  349.3 5.9 %conditional.7 = (f32[12,256]{1,0:T(8,128)S(1)}, f32[12,256]{1,0:T(8,128)S(1)}, f32[256,12,128]{0,2,1:T(8,128)}) conditional(s32[]{:T(128)} %convert_element_type.73, () %tuple.84, (bf16[512,1536]{0,1:T(8,128)(2,1)S(1)}, bf16[256,12,128]{0,2,1:T(8,128)(2,1)S(1)}, bf16[512,1536]{0,1:T(8,128)(2,1)}) %tuple.229), branch_computations={%region_31.31_spmd, %region_32.34_spmd} | conditional | flops 817883136 | bytes 33964140 | solution.py:133
  353.5 1.7 copy.190
  355.2 7.3 %conditional.9 = (f32[12,256]{1,0:T(8,128)S(1)}, f32[12,256]{1,0:T(8,128)S(1)}, f32[256,12,128]{0,2,1:T(8,128)}) conditional(s32[]{:T(128)} %convert_element_type.75, () %tuple.88, (bf16[2,512,1536]{1,2,0:T(8,128)(2,1)}, bf16[256,12,128]{0,2,1:T(8,128)(2,1)S(1)}) %tuple.230), branch_computations={%region_39.39_spmd, %region_40.42_spmd} | conditional | flops 817883136 | bytes 33964112 | solution.py:133
  355.2 2.1 fusion.147
  364.1 46.7 %collective-permute-done.6 = bf16[2,512,1536]{1,2,0:T(8,128)(2,1)} collective-permute-done((bf16[2,512,1536]{1,2,0:T(8,128)(2,1)}, bf16[2,512,1536]{1,2,0:T(8,128)(2,1)}, u32[]{:S(2)}, u32[]{:S(2)}) %collective-permute-start.6) | collective-permute-done | bytes 3145760 | tf_op jit(solution)/shard_map/cond/branch_1_fun/ppermute | solution.py:23
  410.8 7.3 %conditional.6 = (f32[12,256]{1,0:T(8,128)S(1)}, f32[12,256]{1,0:T(8,128)S(1)}, f32[256,12,128]{0,2,1:T(8,128)}) conditional(s32[]{:T(128)} %convert_element_type.72, () %tuple.82, (bf16[2,512,1536]{1,2,0:T(8,128)(2,1)}, bf16[256,12,128]{0,2,1:T(8,128)(2,1)S(1)}) %tuple.232), branch_computations={%region_27.27_spmd, %region_28.30_spmd} | conditional | flops 817883136 | bytes 33964112 | solution.py:133
  410.8 2.1 fusion.145
  416.5 1.6 copy.188
  418.1 44.8 %collective-permute-done.5 = bf16[2,512,1536]{1,2,0:T(8,128)(2,1)} collective-permute-done((bf16[2,512,1536]{1,2,0:T(8,128)(2,1)}, bf16[2,512,1536]{1,2,0:T(8,128)(2,1)}, u32[]{:S(2)}, u32[]{:S(2)}) %collective-permute-start.5) | collective-permute-done | bytes 3145760 | tf_op jit(solution)/shard_map/cond/branch_1_fun/ppermute | solution.py:23
  462.9 7.6 %conditional.5 = (f32[12,256]{1,0:T(8,128)S(1)}, f32[12,256]{1,0:T(8,128)S(1)}, f32[256,12,128]{0,2,1:T(8,128)}) conditional(s32[]{:T(128)} %convert_element_type.71, () %tuple.80, (bf16[2,512,1536]{1,2,0:T(8,128)(2,1)}, bf16[256,12,128]{0,2,1:T(8,128)(2,1)S(1)}) %tuple.233), branch_computations={%region_23.23_spmd, %region_24.26_spmd} | conditional | flops 817883136 | bytes 33964112 | solution.py:133
  463.2 2.1 fusion.144
  470.6 4.8 divide_convert_fusion.1
  475.4 5.2 %fusion.151 = f32[256,3072]{1,0:T(8,128)S(1)} fusion(bf16[256,1536]{0,1:T(8,128)(2,1)S(1)} %bitcast.164, bf16[1536,3072]{1,0:T(8,128)(2,1)} %get-tuple-element.144), kind=kOutput, calls=%fused_computation.176 | convolution fusion | flops 2415919104 | bytes 13369344 | tf_op jit(solution)/shard_map/cond/branch_1_fun/dot_general | solution.py:137
  480.6 1.7 copy-done.1
  483.6 2.6 collective-permute-start.9
  486.2 3.4 add_convert_fusion
  489.9 2.5 add_convert_fusion.1
  (100 shorter events, 40.4 us)
Async XLA Ops:
  2.7 93.4 %copy-start.4 = (bf16[256,1536]{1,0:T(8,128)(2,1)S(1)}, bf16[256,1536]{1,0:T(8,128)(2,1)}, u32[]{:S(2)}) copy-start(bf16[256,1536]{1,0:T(8,128)(2,1)} %refs_2_.1) | copy-start | bytes 2359300
  2.7 93.4 %copy-start.5 = (bf16[256,1536]{1,0:T(8,128)(2,1)S(1)}, bf16[256,1536]{1,0:T(8,128)(2,1)}, u32[]{:S(2)}) copy-start(bf16[256,1536]{1,0:T(8,128)(2,1)} %refs_3_.1) | copy-start | bytes 2359300
  2.7 93.4 %copy-start.27 = (s32[16]{0:T(128)S(1)}, s32[16]{0:T(128)}, u32[]{:S(2)}) copy-start(s32[16]{0:T(128)} %param.37) | copy-start | bytes 196
  2.7 93.4 %copy-start.28 = (s32[16]{0:T(128)S(1)}, s32[16]{0:T(128)}, u32[]{:S(2)}) copy-start(s32[16]{0:T(128)} %param.36) | copy-start | bytes 196
  98.0 170.4 %collective-permute-start.3 = (bf16[2,256,1536]{1,2,0:T(8,128)(2,1)}, bf16[2,256,1536]{1,2,0:T(8,128)(2,1)}, u32[]{:S(2)}, u32[]{:S(2)}) collective-permute-start(bf16[2,256,1536]{1,2,0:T(8,128)(2,1)} %pad_maximum_fusion.1), channel_id=1, source_target_pairs={{4,0},{6,2},{8,4},{10,6},{12,8},{14,10},{16,12},{18,14},{20,16},{2... | collective-permute-start | bytes 4718600 | tf_op jit(solution)/shard_map/cond/branch_1_fun/ppermute | solution.py:23
  99.9 172.6 %collective-permute-start.2 = (bf16[2,256,1536]{1,2,0:T(8,128)(2,1)}, bf16[2,256,1536]{1,2,0:T(8,128)(2,1)}, u32[]{:S(2)}, u32[]{:S(2)}) collective-permute-start(bf16[2,256,1536]{1,2,0:T(8,128)(2,1)} %pad_maximum_fusion.1), channel_id=1, source_target_pairs={{2,0},{4,2},{6,4},{8,6},{10,8},{12,10},{14,12},{16,14},{18,16},{20... | collective-permute-start | bytes 4718600 | tf_op jit(solution)/shard_map/cond/branch_1_fun/ppermute | solution.py:23
  105.1 171.5 %collective-permute-start.1 = (bf16[2,256,1536]{1,2,0:T(8,128)(2,1)}, bf16[2,256,1536]{1,2,0:T(8,128)(2,1)}, u32[]{:S(2)}, u32[]{:S(2)}) collective-permute-start(bf16[2,256,1536]{1,2,0:T(8,128)(2,1)} %pad_maximum_fusion.1), channel_id=1, source_target_pairs={{0,2},{2,4},{4,6},{6,8},{8,10},{10,12},{12,14},{14,16},{16,18},{18... | collective-permute-start | bytes 4718600 | tf_op jit(solution)/shard_map/cond/branch_1_fun/ppermute | solution.py:23
  107.0 209.9 %collective-permute-start = (bf16[2,256,1536]{1,2,0:T(8,128)(2,1)}, bf16[2,256,1536]{1,2,0:T(8,128)(2,1)}, u32[]{:S(2)}, u32[]{:S(2)}) collective-permute-start(bf16[2,256,1536]{1,2,0:T(8,128)(2,1)} %pad_maximum_fusion.1), channel_id=1, source_target_pairs={{0,4},{2,6},{4,8},{6,10},{8,12},{10,14},{12,16},{14,18},{16,20},{1... | collective-permute-start | bytes 4718600 | tf_op jit(solution)/shard_map/cond/branch_1_fun/ppermute | solution.py:23
  117.9 237.3 %collective-permute-start.8 = (bf16[2,512,1536]{1,2,0:T(8,128)(2,1)}, bf16[2,512,1536]{1,2,0:T(8,128)(2,1)}, u32[]{:S(2)}, u32[]{:S(2)}) collective-permute-start(bf16[2,512,1536]{1,2,0:T(8,128)(2,1)} %pad_maximum_fusion), channel_id=1, source_target_pairs={{0,4},{2,6},{4,8},{6,10},{8,12},{10,14},{12,16},{14,18},{16,20},{1... | collective-permute-start | bytes 9437192 | tf_op jit(solution)/shard_map/cond/branch_1_fun/ppermute | solution.py:23
  268.3 94.2 %collective-permute-start.7 = (bf16[2,512,1536]{1,2,0:T(8,128)(2,1)}, bf16[2,512,1536]{1,2,0:T(8,128)(2,1)}, u32[]{:S(2)}, u32[]{:S(2)}) collective-permute-start(bf16[2,512,1536]{1,2,0:T(8,128)(2,1)} %pad_maximum_fusion), channel_id=1, source_target_pairs={{0,2},{2,4},{4,6},{6,8},{8,10},{10,12},{12,14},{14,16},{16,18},{18... | collective-permute-start | bytes 9437192 | tf_op jit(solution)/shard_map/cond/branch_1_fun/ppermute | solution.py:23
  272.6 138.2 %collective-permute-start.6 = (bf16[2,512,1536]{1,2,0:T(8,128)(2,1)}, bf16[2,512,1536]{1,2,0:T(8,128)(2,1)}, u32[]{:S(2)}, u32[]{:S(2)}) collective-permute-start(bf16[2,512,1536]{1,2,0:T(8,128)(2,1)} %pad_maximum_fusion), channel_id=1, source_target_pairs={{2,0},{4,2},{6,4},{8,6},{10,8},{12,10},{14,12},{16,14},{18,16},{20... | collective-permute-start | bytes 9437192 | tf_op jit(solution)/shard_map/cond/branch_1_fun/ppermute | solution.py:23
  276.6 186.3 %collective-permute-start.5 = (bf16[2,512,1536]{1,2,0:T(8,128)(2,1)}, bf16[2,512,1536]{1,2,0:T(8,128)(2,1)}, u32[]{:S(2)}, u32[]{:S(2)}) collective-permute-start(bf16[2,512,1536]{1,2,0:T(8,128)(2,1)} %pad_maximum_fusion), channel_id=1, source_target_pairs={{4,0},{6,2},{8,4},{10,6},{12,8},{14,10},{16,12},{18,14},{20,16},{2... | collective-permute-start | bytes 9437192 | tf_op jit(solution)/shard_map/cond/branch_1_fun/ppermute | solution.py:23
  286.0 1.1 copy-start.6
  290.2 3.6 copy-start.7
  298.8 1.1 copy-start.15
  303.0 3.6 copy-start.16
  309.1 1.1 copy-start.8
  313.4 3.6 copy-start.9
  334.2 3.7 copy-start.3
  337.9 148.3 %collective-permute-start.4 = (f32[512,1536]{1,0:T(8,128)}, f32[512,1536]{1,0:T(8,128)}, u32[]{:S(2)}, u32[]{:S(2)}) collective-permute-start(f32[512,1536]{1,0:T(8,128)} %constant_dynamic-slice_fusion.1), channel_id=1, source_target_pairs={{0,1},{1,0},{2,3},{3,2},{4,5},{5,4},{6,7},{7,6},{8,9},{9,8},{10,11... | collective-permute-start | bytes 9437192 | tf_op jit(solution)/shard_map/cond/branch_1_fun/ppermute | solution.py:144
  350.6 1.1 copy-start.17
  350.6 1.4 copy-start
  353.5 1.7 copy-start.18
  358.3 1.1 copy-start.23
  360.9 1.6 copy-start.24
  413.9 1.1 copy-start.19
  416.5 1.6 copy-start.20
  466.4 1.1 copy-start.21
  468.9 1.6 copy-start.22
  480.6 1.7 copy-start.1
  483.6 6.1 %collective-permute-start.9 = (f32[256,1536]{1,0:T(8,128)}, f32[256,1536]{1,0:T(8,128)}, u32[]{:S(2)}, u32[]{:S(2)}) collective-permute-start(f32[256,1536]{1,0:T(8,128)} %constant_dynamic-slice_fusion), channel_id=1, source_target_pairs={{0,1},{1,0},{2,3},{3,2},{4,5},{5,4},{6,7},{7,6},{8,9},{9,8},{10,11... | collective-permute-start | bytes 4718600 | tf_op jit(solution)/shard_map/cond/branch_1_fun/ppermute | solution.py:144
  486.2 3.7 copy-start.2
  492.7 1.7 copy-start.12
